TPU v7x, 128 devices: a whole 4x4x4 slice. The times are simulated.
128 devices in a mesh: blk: 64 (over z, x, y), col: 2 (over core).
Axes of the slice: x: 4, y: 4, z: 4, core: 2. Of those that a mesh axis runs over, the one named last changes fastest.
Arguments:
- basis_rows: bfloat16 [65536, 4096], P('blk', 'col'), may hold values from -2 to 2
- screen: int32 [64, 4], P('blk'), may hold values from 0 to 1, as said below
Outputs:
- exchange_blocks: float32 [64, 5, 1024, 1024], P('blk', None, 'col')
Inputs may be any that keep to these rules, and one draw needn't show every extreme that they name: `screen`: entries are zero where a + k + 1 >= 64; block 0 keeps all its 4 partners.
All inputs are finite; a program needn't handle non-finite values.
Results may differ from a plain program's by a relative error of at most 0.0003.
Values may be sent and summed in bfloat16 or wider, within the bound.
No kernel may reach another device: no remote copies, remote signals or barrier semaphores. Data moves between devices by JAX's collectives and lax.ppermute only.
A program may use at most 128 MiB of HBM per device.

v0:
```python
import jax
import jax.numpy as jnp
from jax import lax
from jax.sharding import PartitionSpec as P


def shifted(block, axis, distance):
    devices = range(lax.axis_size(axis))
    route = [(i - distance, i) for i in devices if i - distance in devices]
    return lax.ppermute(block, axis, route)


def full_term(own, partner):
    return lax.dot_general(
        own, partner, (((1,), (1,)), ((), ())), preferred_element_type=jnp.float32
    )


def body(basis_rows, screen):
    span = screen.shape[1]
    weights = jnp.concatenate([jnp.ones((1,), jnp.float32), screen[0].astype(jnp.float32)])
    partners = [basis_rows]
    for step in range(1, span + 1):
        partners.append(shifted(basis_rows, "blk", -step))
    terms = jnp.stack([full_term(basis_rows, partner) for partner in partners], axis=0)
    summed = lax.psum_scatter(terms, "col", scatter_dimension=1, tiled=True)
    return (summed * weights[:, None, None])[None]


def solution(mesh):
    return jax.shard_map(
        body,
        mesh=mesh,
        in_specs=(P("blk", "col"), P("blk", None)),
        out_specs=P("blk", None, "col", None),
        check_vma=False,
    )
```

profile of v0, /device:TPU:1, one launch (start us, length us, event | category | flops | bytes accessed | tf_op | source)
XLA Modules:
  0.0 906.6 jit_solution(2824886509004738760)
XLA Ops:
  6.5 0.0 reduce-scatter.2.cloned.1.call-start
  6.5 0.0 copy-start
  6.5 1.5 collective-permute-start
  8.1 1.3 collective-permute-start.1
  9.4 1.3 collective-permute-start.2
  10.7 1.3 collective-permute-start.3
  12.0 9.9 %bitcast_dynamic-update-slice_fusion.4 = f32[5,1024,1024]{2,1,0:T(8,128)} fusion(bf16[1024,2048]{1,0:T(8,128)(2,1)} %param.2), kind=kOutput, calls=%fused_computation.5 | convolution fusion | flops 4294967296 | bytes 12582912 | tf_op jit(solution)/shard_map/dot_general | solution.py:14
  21.9 168.9 %collective-permute-done = bf16[1024,2048]{1,0:T(8,128)(2,1)S(1)} collective-permute-done((bf16[1024,2048]{1,0:T(8,128)(2,1)}, bf16[1024,2048]{1,0:T(8,128)(2,1)S(1)}, u32[]{:S(2)}, u32[]{:S(2)}) %collective-permute-start) | collective-permute-done | bytes 4194336 | tf_op jit(solution)/shard_map/ppermute | solution.py:10
  190.8 0.0 copy-done
  190.8 6.1 bitcast_dynamic-update-slice_fusion.3
  196.9 0.0 collective-permute-done.1
  196.9 6.1 bitcast_dynamic-update-slice_fusion.2
  203.0 0.0 collective-permute-done.2
  203.1 6.1 bitcast_dynamic-update-slice_fusion.1
  209.2 324.3 %collective-permute-done.3 = bf16[1024,2048]{1,0:T(8,128)(2,1)S(1)} collective-permute-done((bf16[1024,2048]{1,0:T(8,128)(2,1)}, bf16[1024,2048]{1,0:T(8,128)(2,1)S(1)}, u32[]{:S(2)}, u32[]{:S(2)}) %collective-permute-start.3) | collective-permute-done | bytes 4194336 | tf_op jit(solution)/shard_map/ppermute | solution.py:10
  533.5 6.1 bitcast_dynamic-update-slice_fusion
  539.5 0.0 copy-start.1
  539.5 0.0 reduce-scatter.2.cloned.1.call-update
  539.6 0.6 copy-done.1
  540.2 0.1 pad_maximum_fusion
  540.3 348.9 %reduce-scatter.2.cloned.1.call-done = f32[5,512,1024]{2,1,0:T(8,128)} async-done(((f32[5,1024,1024]{2,1,0:T(8,128)}), f32[5,512,1024]{2,1,0:T(8,128)}) %reduce-scatter.2.cloned.1.call-update) | async-done | bytes 10485776 | tf_op jit(solution)/shard_map/reduce_scatter | solution.py:26
  889.2 10.6 %multiply_bitcast_fusion = f32[1,5,512,1024]{3,2,1,0:T(8,128)} fusion(f32[5,512,1024]{2,1,0:T(8,128)} %reduce-scatter.2.cloned.1.call-done, f32[5]{0:T(128)S(1)} %pad_maximum_fusion), kind=kLoop, calls=%fused_computation | loop fusion | flops 2621440 | bytes 20971540 | tf_op jit(solution)/shard_map/broadcast_in_dim | solution.py:27
  (1 shorter events, 0.0 us)
Async XLA Ops:
  6.5 882.6 %reduce-scatter.2.cloned.1.call-start = ((), (), s32[]{:S(2)}) async-start(), calls=%async_computation.1 | async-start | bytes 31457280 | tf_op jit(solution)/shard_map/reduce_scatter | solution.py:26
  6.5 184.3 %copy-start = (bf16[1024,2048]{1,0:T(8,128)(2,1)S(1)}, bf16[1024,2048]{1,0:T(8,128)(2,1)}, u32[]{:S(2)}) copy-start(bf16[1024,2048]{1,0:T(8,128)(2,1)} %param.2) | copy-start | bytes 12582916
  6.5 184.3 %collective-permute-start = (bf16[1024,2048]{1,0:T(8,128)(2,1)}, bf16[1024,2048]{1,0:T(8,128)(2,1)S(1)}, u32[]{:S(2)}, u32[]{:S(2)}) collective-permute-start(bf16[1024,2048]{1,0:T(8,128)(2,1)} %param.2), channel_id=1, source_target_pairs={{2,0},{4,2},{6,4},{8,6},{10,8},{12,10},{14,12},{16,14},{18,16},{20... | collective-permute-start | bytes 12582920 | tf_op jit(solution)/shard_map/ppermute | solution.py:10
  8.1 188.8 %collective-permute-start.1 = (bf16[1024,2048]{1,0:T(8,128)(2,1)}, bf16[1024,2048]{1,0:T(8,128)(2,1)S(1)}, u32[]{:S(2)}, u32[]{:S(2)}) collective-permute-start(bf16[1024,2048]{1,0:T(8,128)(2,1)} %param.2), channel_id=1, source_target_pairs={{4,0},{6,2},{8,4},{10,6},{12,8},{14,10},{16,12},{18,14},{20,16},{2... | collective-permute-start | bytes 12582920 | tf_op jit(solution)/shard_map/ppermute | solution.py:10
  9.4 193.7 %collective-permute-start.2 = (bf16[1024,2048]{1,0:T(8,128)(2,1)}, bf16[1024,2048]{1,0:T(8,128)(2,1)S(1)}, u32[]{:S(2)}, u32[]{:S(2)}) collective-permute-start(bf16[1024,2048]{1,0:T(8,128)(2,1)} %param.2), channel_id=1, source_target_pairs={{6,0},{8,2},{10,4},{12,6},{14,8},{16,10},{18,12},{20,14},{22,16},{... | collective-permute-start | bytes 12582920 | tf_op jit(solution)/shard_map/ppermute | solution.py:10
  10.7 522.8 %collective-permute-start.3 = (bf16[1024,2048]{1,0:T(8,128)(2,1)}, bf16[1024,2048]{1,0:T(8,128)(2,1)S(1)}, u32[]{:S(2)}, u32[]{:S(2)}) collective-permute-start(bf16[1024,2048]{1,0:T(8,128)(2,1)} %param.2), channel_id=1, source_target_pairs={{8,0},{10,2},{12,4},{14,6},{16,8},{18,10},{20,12},{22,14},{24,16},... | collective-permute-start | bytes 12582920 | tf_op jit(solution)/shard_map/ppermute | solution.py:10
  539.5 0.7 copy-start.1
Sparse Core Ops, SparseCore 0:
  539.7 349.4 reduce-scatter.1
where the time goes:
time: 907 us
  waiting for transfers between devices  842 us (93%)
  matrix products  34.4 us (4%)
  between operations  13.4 us (1%)
  other arithmetic  10.6 us (1%)
    ppermute x4, waiting for transfers between devices, shifted(): return lax.ppermute(block, axis, route)  493 us
    reduce_scatter x1, waiting for transfers between devices, body(): summed = lax.psum_scatter(terms, 'col', scatter_dimension=1, tiled=True)  349 us
    dot_general x5, matrix products, full_term(): lax.dot_general(own, partner, (((1,), (1,)), ((), ())), preferred_element...  34.4 us
  transfers between devices with their start and end apart: 5, of which 3 were waited for; matrix products, arithmetic and copies ran while one was open for 3% of the time, Pallas kernels for 0%

commit v1 on v0

v1 whole, which is shorter than its diff:
```python
import jax
import jax.numpy as jnp
from jax import lax
from jax.experimental import pallas as pl
from jax.experimental.pallas import tpu as pltpu
from jax.sharding import PartitionSpec as P

RING = 4
STRIP = 256
MIB = 1 << 20
SMALL = pl.CostEstimate(flops=1, bytes_accessed=1, transcendentals=0)
VMEM = pl.BlockSpec(memory_space=pltpu.VMEM)
SMEM = pl.BlockSpec(memory_space=pltpu.SMEM)
ANY = pl.BlockSpec(memory_space=pl.ANY)


def product(rows, partner):
    return lax.dot_general(
        rows, partner, (((1,), (1,)), ((), ())), preferred_element_type=jnp.float32
    )


def handed_products(handed, partners):
    height, counts = handed.shape[0], [p.shape[0] for p in partners]

    def kernel(handed_ref, *refs):
        *partner_refs, made_ref = refs

        @pl.loop(0, height // STRIP)
        def _(strip):
            at = pl.ds(pl.multiple_of(strip * STRIP, STRIP), STRIP)
            first = 0
            for ref, count in zip(partner_refs, counts):
                made_ref[at, first:first + count] = product(handed_ref[at, :], ref[...])
                first += count

    return pl.pallas_call(
        kernel,
        out_shape=jax.ShapeDtypeStruct((height, sum(counts)), jnp.float32),
        in_specs=[VMEM] * (1 + len(partners)),
        out_specs=VMEM,
        compiler_params=pltpu.CompilerParams(vmem_limit_bytes=20 * MIB),
        cost_estimate=SMALL,
    )(handed, *partners)


def kept_products(out, weights, kept, theirs, partners, places, shape):
    height, counts = kept.shape[0], [p.shape[0] for p in partners]

    def kernel(weights_ref, kept_ref, theirs_ref, *refs):
        refs = list(refs)
        partner_refs, refs = refs[:len(partners)], refs[len(partners):]
        if out is not None:
            refs = refs[1:]
        out_ref, made_ref, sems = refs

        copies, first = [], 0
        for index, (ref, (k, column, _), count) in enumerate(zip(partner_refs, places, counts)):
            across = pl.ds(first, count)

            @pl.loop(0, height // STRIP)
            def _(strip):
                at = pl.ds(pl.multiple_of(strip * STRIP, STRIP), STRIP)
                total = product(kept_ref[at, :], ref[...]) + theirs_ref[at, across]
                made_ref[at, across] = total * weights_ref[k]

            copy = pltpu.make_async_copy(
                made_ref.at[:, across], out_ref.at[k, :, pl.ds(column, count)], sems.at[index]
            )
            copy.start()
            copies.append(copy)
            first += count
        for copy in copies:
            copy.wait()

    first_call = out is None
    return pl.pallas_call(
        kernel,
        out_shape=jax.ShapeDtypeStruct(shape, jnp.float32),
        in_specs=[SMEM] + [VMEM] * (2 + len(partners)) + ([] if first_call else [ANY]),
        out_specs=ANY,
        scratch_shapes=[
            pltpu.VMEM((height, sum(counts)), jnp.float32),
            pltpu.SemaphoreType.DMA((len(partners),)),
        ],
        input_output_aliases={} if first_call else {3 + len(partners): 0},
        compiler_params=pltpu.CompilerParams(vmem_limit_bytes=20 * MIB),
        cost_estimate=SMALL,
    )(weights, kept, theirs, *partners, *([] if first_call else [out]))


def body(basis_rows, screen):
    blocks = lax.axis_size("blk")
    height = basis_rows.shape[0]
    half = height // 2
    column = lax.axis_index("blk") % RING
    core = lax.axis_index("col")
    weights = jnp.concatenate([jnp.ones((1,), jnp.float32), screen[0].astype(jnp.float32)])

    def below(distance):
        return [(i, (i - distance) % blocks) for i in range(blocks)]

    def around(distance):
        return [(i, i - i % RING + (i + distance) % RING) for i in range(blocks)]

    def rows(array, first, count):
        return lax.slice_in_dim(array, first, first + count, axis=0)

    q = height // 4
    phases = [
        dict(send=[("4", 0, q)], make=[(0, 0, height)]),
        dict(send=[("4", q, q), ("1", 0, q), ("3", 0, q)], make=[(4, 0, q)]),
        dict(send=[("4", 2 * q, q), ("1", q, q), ("3", q, q)], make=[(4, q, q), (1, 0, q), (3, 0, q)]),
        dict(send=[("4", 3 * q, q), ("1", 2 * q, q), ("3", 2 * q, q)], make=[(4, 2 * q, q), (1, q, q), (3, q, q)]),
        dict(send=[("1", 3 * q, q), ("3", 3 * q, q)], make=[(4, 3 * q, q), (1, 2 * q, q), (3, 2 * q, q)]),
        dict(send=[("2-", 2 * q, q), ("2+", 0, q)], make=[(1, 3 * q, q), (3, 3 * q, q)]),
        dict(send=[("2-", 3 * q, q), ("2+", q, q)], make=[(2, 2 * q, q), (2, 0, q)]),
        dict(send=[], make=[(2, 3 * q, q), (2, q, q)]),
    ]

    own = basis_rows
    kept = lax.dynamic_slice_in_dim(own, core * half, half, 0)
    handed = lax.dynamic_slice_in_dim(own, (1 - core) * half, half, 0)
    out = None
    held = {0: {(0, height): own}, 1: {}, 2: {}, 3: {}, 4: {}}
    ready = {}

    def part(k, first, count):
        for (start, size), array in held[k].items():
            if start <= first and first + count <= start + size:
                return rows(array, first - start, count)
        raise KeyError

    def operand(how, first, count):
        if how == "4":
            return part(0, first, count)
        if how == "1":
            return jnp.where(column == 0, part(4, first, count), part(0, first, count))
        if how == "3":
            return jnp.where(column == RING - 1, part(0, first, count), part(4, first, count))
        return part(1 if how == "2-" else 3, first, count)

    routes = {
        "4": (4, below(4)), "1": (1, around(-1)),
        "3": (3, around(1)), "2-": (2, below(1)), "2+": (2, below(-1)),
    }

    across = [(0, 1), (1, 0)]
    made, waiting = None, None
    for index, phase in enumerate(phases):
        last = index + 1 == len(phases)
        arrived = {}
        for how, first, count in phase["send"]:
            k, route = routes[how]
            send = ready.pop((how, first, count), None)
            if send is None:
                send = operand(how, first, count)
            arrived[k, first, count] = lax.ppermute(send, "blk", route)
        if made is not None:
            theirs = lax.ppermute(made, "col", across)
            partners = [part(*piece) for piece in waiting]
            out = kept_products(out, weights, kept, theirs, partners, waiting, (5, half, height))
        waiting = phase["make"]
        made = handed_products(handed, [part(*piece) for piece in waiting])
        if last:
            break
        for how, first, count in phases[index + 1]["send"]:
            if how == "4":
                ready[how, first, count] = operand(how, first, count)
        for (k, first, count), array in arrived.items():
            held[k][first, count] = array
        state = (held, ready, kept, handed, made, out)
        held, ready, kept, handed, made, out = lax.optimization_barrier(state)
    theirs = lax.ppermute(made, "col", across)
    partners = [part(*piece) for piece in waiting]
    out = kept_products(out, weights, kept, theirs, partners, waiting, (5, half, height))
    return out[None]


def solution(mesh):
    return jax.shard_map(
        body,
        mesh=mesh,
        in_specs=(P("blk", "col"), P("blk", None)),
        out_specs=P("blk", None, "col", None),
        check_vma=False,
    )
```

time: 907 us -> 229 us (0.25)
  waiting for transfers between devices: 842 us -> 116 us
  starting transfers between devices: 5.42 us -> 56.7 us
  Pallas kernels: 0 us -> 45.6 us
  matrix products: 34.4 us -> 0 us
  between operations: 13.4 us -> 0.4 us
    ppermute x4 -> x24, waiting for transfers between devices: 493 us -> 116 us  [the longest x16 116 us: body(): arrived[k, first, count] = lax.ppermute(send, 'blk', route)]
    reduce_scatter x1 -> x0, waiting for transfers between devices: 349 us -> none  [body(): summed = lax.psum_scatter(terms, 'col', scatter_dimension=1, tiled=True)]
    ppermute x4 -> x24, starting transfers between devices: 5.42 us -> 56.7 us  [the longest x16 46.5 us: body(): arrived[k, first, count] = lax.ppermute(send, 'blk', route)]
    pallas_call x0 -> x16, Pallas kernels: none -> 45.6 us  [the longest x8 30.3 us: kept_products(): pl.pallas_call(kernel, out_shape=jax.ShapeDtypeStruct(shape, jnp.float32)...]
    dot_general x5 -> x0, matrix products: 34.4 us -> none  [full_term(): lax.dot_general(own, partner, (((1,), (1,)), ((), ())), preferred_element...]
    broadcast_in_dim x1 -> x0, other arithmetic: 10.6 us -> none  [body(): return (summed * weights[:, None, None])[None]]
  transfers between devices with their start and end apart: 5 -> 24, of which waited for: 3 -> 14; matrix products, arithmetic and copies ran while one was open for 3% -> 3% of each run, Pallas kernels for 0% -> 18%
where the time goes in v1:
time: 229 us
  waiting for transfers between devices  116 us (51%)
  starting transfers between devices  56.7 us (25%)
  Pallas kernels  45.6 us (20%)
  local copies, waits for them, and re-layouts  7.32 us (3%)
  other arithmetic  2.47 us (1%)
    ppermute x16, waiting for transfers between devices, body(): arrived[k, first, count] = lax.ppermute(send, 'blk', route)  116 us
    ppermute x16, starting transfers between devices, body(): arrived[k, first, count] = lax.ppermute(send, 'blk', route)  46.5 us
    pallas_call x8, Pallas kernels, kept_products(): pl.pallas_call(kernel, out_shape=jax.ShapeDtypeStruct(shape, jnp.float32)...  30.3 us
    pallas_call x8, Pallas kernels, handed_products(): pl.pallas_call(kernel, out_shape=jax.ShapeDtypeStruct((height, sum(counts...  15.3 us
    ppermute x8, starting transfers between devices, body(): theirs = lax.ppermute(made, 'col', across)  10.2 us
  transfers between devices with their start and end apart: 24, of which 14 were waited for; matrix products, arithmetic and copies ran while one was open for 3% of the time, Pallas kernels for 18%

profile of v1, /device:TPU:1, one launch (start us, length us, event | category | flops | bytes accessed | tf_op | source)
XLA Modules:
  0.0 229.0 jit_solution(10995587257545463642)
XLA Ops:
  0.0 3.2 %fusion = (bf16[256,2048]{1,0:T(8,128)(2,1)}, bf16[256,2048]{1,0:T(8,128)(2,1)}) fusion(bf16[1024,2048]{1,0:T(8,128)(2,1)} %refs_0_.2), kind=kLoop, calls=%fused_computation.12 | loop fusion | bytes 4194304 | tf_op jit(solution)/shard_map/slice | solution.py:107
  3.2 6.8 %collective-permute-start = (bf16[256,2048]{1,0:T(8,128)(2,1)}, bf16[256,2048]{1,0:T(8,128)(2,1)S(1)}, u32[]{:S(2)}, u32[]{:S(2)}) collective-permute-start(bf16[256,2048]{1,0:T(8,128)(2,1)} %get-tuple-element.154), channel_id=1, source_target_pairs={{0,120},{2,122},{4,124},{6,126},{8,0},{10,2},{12,4},{14,6},{16,8},... | collective-permute-start | bytes 3145736 | tf_op jit(solution)/shard_map/ppermute | solution.py:158
  9.9 4.1 %constant_dynamic-slice_fusion = (bf16[512,2048]{1,0:T(8,128)(2,1)S(1)}, bf16[512,2048]{1,0:T(8,128)(2,1)}) fusion(bf16[1024,2048]{1,0:T(8,128)(2,1)} %refs_0_.2, s32[]{:T(128)S(6)} %select_n.52, s32[]{:T(128)S(6)} %select_n.51), kind=kLoop, calls=%fused_computation.9 | loop fusion | bytes 8388616 | tf_op jit(solution)/shard_map/dynamic_slice | solution.py:123
  14.1 3.9 %shard_map.28 = f32[512,1024]{1,0:T(8,128)} custom-call(bf16[512,2048]{1,0:T(8,128)(2,1)S(1)} %get-tuple-element.134.handed_ref, bf16[1024,2048]{1,0:T(8,128)(2,1)S(1)} %copy-done.1), custom_call_target="tpu_custom_call" | custom-call | flops 1 | bytes 1 | tf_op jit(solution)/shard_map/pallas_call | solution.py:37
  18.0 14.1 %collective-permute-done.refs_0_ = bf16[256,2048]{1,0:T(8,128)(2,1)S(1)} collective-permute-done((bf16[256,2048]{1,0:T(8,128)(2,1)}, bf16[256,2048]{1,0:T(8,128)(2,1)S(1)}, u32[]{:S(2)}, u32[]{:S(2)}) %collective-permute-start) | collective-permute-done | bytes 1048608 | tf_op jit(solution)/shard_map/ppermute | solution.py:158
  35.5 2.8 %collective-permute-start.1 = (bf16[256,2048]{1,0:T(8,128)(2,1)S(1)}, bf16[256,2048]{1,0:T(8,128)(2,1)S(1)}, u32[]{:S(2)}, u32[]{:S(2)}) collective-permute-start(bf16[256,2048]{1,0:T(8,128)(2,1)S(1)} %get-tuple-element.148), channel_id=1, source_target_pairs={{0,6},{2,0},{4,2},{6,4},{8,14},{10,8},{12,10},{14,12},{16,22},{18,... | collective-permute-start | bytes 3145736 | tf_op jit(solution)/shard_map/ppermute | solution.py:158
  38.3 5.4 %collective-permute-start.3 = (bf16[256,2048]{1,0:T(8,128)(2,1)}, bf16[256,2048]{1,0:T(8,128)(2,1)S(1)}, u32[]{:S(2)}, u32[]{:S(2)}) collective-permute-start(bf16[256,2048]{1,0:T(8,128)(2,1)} %get-tuple-element.75), channel_id=1, source_target_pairs={{0,120},{2,122},{4,124},{6,126},{8,0},{10,2},{12,4},{14,6},{16,8},... | collective-permute-start | bytes 3145736 | tf_op jit(solution)/shard_map/ppermute | solution.py:158
  44.8 5.5 %shard_map.30.refs_1_ = f32[5,512,1024]{2,1,0:T(8,128)} custom-call(f32[5]{0:T(128)S(1)} %pad_maximum_fusion.weights_ref, bf16[512,2048]{1,0:T(8,128)(2,1)S(1)} %copy-done, f32[512,1024]{1,0:T(8,128)} %collective-permute-done.4.theirs_ref, bf16[1024,2048]{1,0:T(8,128)(2,1)S(1)} %copy-done.2), custom_call_target="tpu_custom_call" | custom-call | flops 1 | bytes 1 | tf_op jit(solution)/shard_map/pallas_call | solution.py:77
  50.4 10.6 %collective-permute-done.1.refs_1_ = bf16[256,2048]{1,0:T(8,128)(2,1)S(1)} collective-permute-done((bf16[256,2048]{1,0:T(8,128)(2,1)S(1)}, bf16[256,2048]{1,0:T(8,128)(2,1)S(1)}, u32[]{:S(2)}, u32[]{:S(2)}) %collective-permute-start.1) | collective-permute-done | bytes 1048608 | tf_op jit(solution)/shard_map/ppermute | solution.py:158
  60.9 3.1 %collective-permute-done.2.refs_2_ = bf16[256,2048]{1,0:T(8,128)(2,1)S(1)} collective-permute-done((bf16[256,2048]{1,0:T(8,128)(2,1)S(1)}, bf16[256,2048]{1,0:T(8,128)(2,1)S(1)}, u32[]{:S(2)}, u32[]{:S(2)}) %collective-permute-start.2) | collective-permute-done | bytes 1048608 | tf_op jit(solution)/shard_map/ppermute | solution.py:158
  64.0 2.3 %collective-permute-done.3.refs_0_ = bf16[256,2048]{1,0:T(8,128)(2,1)S(1)} collective-permute-done((bf16[256,2048]{1,0:T(8,128)(2,1)}, bf16[256,2048]{1,0:T(8,128)(2,1)S(1)}, u32[]{:S(2)}, u32[]{:S(2)}) %collective-permute-start.3) | collective-permute-done | bytes 1048608 | tf_op jit(solution)/shard_map/ppermute | solution.py:158
  66.6 2.4 %collective-permute-start.5 = (bf16[256,2048]{1,0:T(8,128)(2,1)S(1)}, bf16[256,2048]{1,0:T(8,128)(2,1)S(1)}, u32[]{:S(2)}, u32[]{:S(2)}) collective-permute-start(bf16[256,2048]{1,0:T(8,128)(2,1)S(1)} %get-tuple-element.146), channel_id=1, source_target_pairs={{0,6},{2,0},{4,2},{6,4},{8,14},{10,8},{12,10},{14,12},{16,22},{18,... | collective-permute-start | bytes 3145736 | tf_op jit(solution)/shard_map/ppermute | solution.py:158
  69.0 5.4 %collective-permute-start.7 = (bf16[256,2048]{1,0:T(8,128)(2,1)S(1)}, bf16[256,2048]{1,0:T(8,128)(2,1)S(1)}, u32[]{:S(2)}, u32[]{:S(2)}) collective-permute-start(bf16[256,2048]{1,0:T(8,128)(2,1)S(1)} %get-tuple-element.84), channel_id=1, source_target_pairs={{0,120},{2,122},{4,124},{6,126},{8,0},{10,2},{12,4},{14,6},{16,8},... | collective-permute-start | bytes 3145736 | tf_op jit(solution)/shard_map/ppermute | solution.py:158
  78.4 2.3 %shard_map.32.refs_3_ = f32[5,512,1024]{2,1,0:T(8,128)} custom-call(f32[5]{0:T(128)S(1)} %pad_maximum_fusion.weights_ref, bf16[512,2048]{1,0:T(8,128)(2,1)S(1)} %copy-done, f32[512,256]{1,0:T(8,128)S(1)} %collective-permute-done.8.theirs_ref, bf16[256,2048]{1,0:T(8,128)(2,1)S(1)} %collective-permute-done.refs_0_, ...), custom_call_target="tpu_custom_call", output_to_operand_aliasing={{}: (4, {})} | custom-call | flops 1 | bytes 1 | tf_op jit(solution)/shard_map/pallas_call | solution.py:77
  80.7 9.4 %collective-permute-done.5.refs_1_ = bf16[256,2048]{1,0:T(8,128)(2,1)S(1)} collective-permute-done((bf16[256,2048]{1,0:T(8,128)(2,1)S(1)}, bf16[256,2048]{1,0:T(8,128)(2,1)S(1)}, u32[]{:S(2)}, u32[]{:S(2)}) %collective-permute-start.5) | collective-permute-done | bytes 1048608 | tf_op jit(solution)/shard_map/ppermute | solution.py:158
  90.2 3.0 %collective-permute-done.6.refs_2_ = bf16[256,2048]{1,0:T(8,128)(2,1)S(1)} collective-permute-done((bf16[256,2048]{1,0:T(8,128)(2,1)S(1)}, bf16[256,2048]{1,0:T(8,128)(2,1)S(1)}, u32[]{:S(2)}, u32[]{:S(2)}) %collective-permute-start.6) | collective-permute-done | bytes 1048608 | tf_op jit(solution)/shard_map/ppermute | solution.py:158
  95.2 2.6 %collective-permute-start.12 = (f32[512,768]{1,0:T(8,128)S(1)}, f32[512,768]{1,0:T(8,128)S(1)}, u32[]{:S(2)}, u32[]{:S(2)}) collective-permute-start(f32[512,768]{1,0:T(8,128)S(1)} %shard_map.31), channel_id=1, source_target_pairs={{0,1},{1,0},{2,3},{3,2},{4,5},{5,4},{6,7},{7,6},{8,9},{9,8},{10,11... | collective-permute-start | bytes 4718600 | tf_op jit(solution)/shard_map/ppermute | solution.py:160
  98.0 2.7 %collective-permute-start.9 = (bf16[256,2048]{1,0:T(8,128)(2,1)S(1)}, bf16[256,2048]{1,0:T(8,128)(2,1)S(1)}, u32[]{:S(2)}, u32[]{:S(2)}) collective-permute-start(bf16[256,2048]{1,0:T(8,128)(2,1)S(1)} %get-tuple-element.144), channel_id=1, source_target_pairs={{0,6},{2,0},{4,2},{6,4},{8,14},{10,8},{12,10},{14,12},{16,22},{18,... | collective-permute-start | bytes 3145736 | tf_op jit(solution)/shard_map/ppermute | solution.py:158
  100.7 5.5 %collective-permute-start.11 = (bf16[256,2048]{1,0:T(8,128)(2,1)S(1)}, bf16[256,2048]{1,0:T(8,128)(2,1)S(1)}, u32[]{:S(2)}, u32[]{:S(2)}) collective-permute-start(bf16[256,2048]{1,0:T(8,128)(2,1)S(1)} %get-tuple-element.96), channel_id=1, source_target_pairs={{0,120},{2,122},{4,124},{6,126},{8,0},{10,2},{12,4},{14,6},{16,8},... | collective-permute-start | bytes 3145736 | tf_op jit(solution)/shard_map/ppermute | solution.py:158
  108.3 4.2 %shard_map.34.refs_3_ = f32[5,512,1024]{2,1,0:T(8,128)} custom-call(f32[5]{0:T(128)S(1)} %pad_maximum_fusion.weights_ref, bf16[512,2048]{1,0:T(8,128)(2,1)S(1)} %copy-done, f32[512,768]{1,0:T(8,128)S(1)} %collective-permute-done.12.theirs_ref, bf16[256,2048]{1,0:T(8,128)(2,1)S(1)} %collective-permute-done.3.refs_0_, ...), custom_call_target="tpu_custom_call", output_to_operand_aliasing={{}: (6, {})} | custom-call | flops 1 | bytes 1 | tf_op jit(solution)/shard_map/pallas_call | solution.py:77
  112.5 11.5 %collective-permute-done.10.refs_2_ = bf16[256,2048]{1,0:T(8,128)(2,1)S(1)} collective-permute-done((bf16[256,2048]{1,0:T(8,128)(2,1)S(1)}, bf16[256,2048]{1,0:T(8,128)(2,1)S(1)}, u32[]{:S(2)}, u32[]{:S(2)}) %collective-permute-start.10) | collective-permute-done | bytes 1048608 | tf_op jit(solution)/shard_map/ppermute | solution.py:158
  124.0 4.3 %collective-permute-done.11.refs_0_ = bf16[256,2048]{1,0:T(8,128)(2,1)S(1)} collective-permute-done((bf16[256,2048]{1,0:T(8,128)(2,1)S(1)}, bf16[256,2048]{1,0:T(8,128)(2,1)S(1)}, u32[]{:S(2)}, u32[]{:S(2)}) %collective-permute-start.11) | collective-permute-done | bytes 1048608 | tf_op jit(solution)/shard_map/ppermute | solution.py:158
  133.4 4.3 %shard_map.36.refs_3_ = f32[5,512,1024]{2,1,0:T(8,128)} custom-call(f32[5]{0:T(128)S(1)} %pad_maximum_fusion.weights_ref, bf16[512,2048]{1,0:T(8,128)(2,1)S(1)} %copy-done, f32[512,768]{1,0:T(8,128)S(1)} %collective-permute-done.15.theirs_ref, bf16[256,2048]{1,0:T(8,128)(2,1)S(1)} %collective-permute-done.7.refs_0_, ...), custom_call_target="tpu_custom_call", output_to_operand_aliasing={{}: (6, {})} | custom-call | flops 1 | bytes 1 | tf_op jit(solution)/shard_map/pallas_call | solution.py:77
  137.6 17.0 %collective-permute-done.13.refs_0_ = bf16[256,2048]{1,0:T(8,128)(2,1)S(1)} collective-permute-done((bf16[256,2048]{1,0:T(8,128)(2,1)S(1)}, bf16[256,2048]{1,0:T(8,128)(2,1)S(1)}, u32[]{:S(2)}, u32[]{:S(2)}) %collective-permute-start.13) | collective-permute-done | bytes 1048608 | tf_op jit(solution)/shard_map/ppermute | solution.py:158
  158.0 6.9 %collective-permute-start.17 = (bf16[256,2048]{1,0:T(8,128)(2,1)S(1)}, bf16[256,2048]{1,0:T(8,128)(2,1)S(1)}, u32[]{:S(2)}, u32[]{:S(2)}) collective-permute-start(bf16[256,2048]{1,0:T(8,128)(2,1)S(1)} %collective-permute-done.9.refs_1_), channel_id=1, source_target_pairs={{0,126},{2,0},{4,2},{6,4},{8,6},{10,8},{12,10},{14,12},{16,14},{18... | collective-permute-start | bytes 3145736 | tf_op jit(solution)/shard_map/ppermute | solution.py:158
  166.4 4.2 %shard_map.38.refs_2_ = f32[5,512,1024]{2,1,0:T(8,128)} custom-call(f32[5]{0:T(128)S(1)} %pad_maximum_fusion.weights_ref, bf16[512,2048]{1,0:T(8,128)(2,1)S(1)} %copy-done, f32[512,768]{1,0:T(8,128)S(1)} %collective-permute-done.18.theirs_ref, bf16[256,2048]{1,0:T(8,128)(2,1)S(1)} %collective-permute-done.11.refs_0_, ...), custom_call_target="tpu_custom_call", output_to_operand_aliasing={{}: (6, {})} | custom-call | flops 1 | bytes 1 | tf_op jit(solution)/shard_map/pallas_call | solution.py:77
  170.6 17.6 %collective-permute-done.16.refs_1_ = bf16[256,2048]{1,0:T(8,128)(2,1)S(1)} collective-permute-done((bf16[256,2048]{1,0:T(8,128)(2,1)S(1)}, bf16[256,2048]{1,0:T(8,128)(2,1)S(1)}, u32[]{:S(2)}, u32[]{:S(2)}) %collective-permute-start.16) | collective-permute-done | bytes 1048608 | tf_op jit(solution)/shard_map/ppermute | solution.py:158
  189.0 6.9 %collective-permute-start.20 = (bf16[256,2048]{1,0:T(8,128)(2,1)S(1)}, bf16[256,2048]{1,0:T(8,128)(2,1)S(1)}, u32[]{:S(2)}, u32[]{:S(2)}) collective-permute-start(bf16[256,2048]{1,0:T(8,128)(2,1)S(1)} %collective-permute-done.13.refs_0_), channel_id=1, source_target_pairs={{0,126},{2,0},{4,2},{6,4},{8,6},{10,8},{12,10},{14,12},{16,14},{18... | collective-permute-start | bytes 3145736 | tf_op jit(solution)/shard_map/ppermute | solution.py:158
  197.4 3.2 %shard_map.40.refs_2_ = f32[5,512,1024]{2,1,0:T(8,128)} custom-call(f32[5]{0:T(128)S(1)} %pad_maximum_fusion.weights_ref, bf16[512,2048]{1,0:T(8,128)(2,1)S(1)} %copy-done, f32[512,512]{1,0:T(8,128)S(1)} %collective-permute-done.21.theirs_ref, bf16[256,2048]{1,0:T(8,128)(2,1)S(1)} %collective-permute-done.13.refs_0_, ...), custom_call_target="tpu_custom_call", output_to_operand_aliasing={{}: (5, {})} | custom-call | flops 1 | bytes 1 | tf_op jit(solution)/shard_map/pallas_call | solution.py:77
  200.7 18.6 %collective-permute-done.19.refs_1_ = bf16[256,2048]{1,0:T(8,128)(2,1)S(1)} collective-permute-done((bf16[256,2048]{1,0:T(8,128)(2,1)S(1)}, bf16[256,2048]{1,0:T(8,128)(2,1)S(1)}, u32[]{:S(2)}, u32[]{:S(2)}) %collective-permute-start.19) | collective-permute-done | bytes 1048608 | tf_op jit(solution)/shard_map/ppermute | solution.py:158
  222.3 3.3 %shard_map.42.refs_2_ = f32[5,512,1024]{2,1,0:T(8,128)} custom-call(f32[5]{0:T(128)S(1)} %pad_maximum_fusion.weights_ref, bf16[512,2048]{1,0:T(8,128)(2,1)S(1)} %copy-done, f32[512,512]{1,0:T(8,128)S(1)} %collective-permute-done.23.theirs_ref, bf16[256,2048]{1,0:T(8,128)(2,1)S(1)} %collective-permute-done.17.refs_0_, ...), custom_call_target="tpu_custom_call", output_to_operand_aliasing={{}: (5, {})} | custom-call | flops 1 | bytes 1 | tf_op jit(solution)/shard_map/pallas_call | solution.py:77
  225.6 3.3 %shard_map.43 = f32[5,512,1024]{2,1,0:T(8,128)} custom-call(f32[5]{0:T(128)S(1)} %pad_maximum_fusion.weights_ref, bf16[512,2048]{1,0:T(8,128)(2,1)S(1)} %copy-done, f32[512,512]{1,0:T(8,128)S(1)} %collective-permute-done.22.theirs_ref, bf16[256,2048]{1,0:T(8,128)(2,1)S(1)} %collective-permute-done.20.refs_0_, ...), custom_call_target="tpu_custom_call", output_to_operand_aliasing={{}: (5, {})} | custom-call | flops 1 | bytes 1 | tf_op jit(solution)/shard_map/pallas_call | solution.py:77
  (48 shorter events, 28.2 us)
Async XLA Ops:
  3.2 28.9 %collective-permute-start = (bf16[256,2048]{1,0:T(8,128)(2,1)}, bf16[256,2048]{1,0:T(8,128)(2,1)S(1)}, u32[]{:S(2)}, u32[]{:S(2)}) collective-permute-start(bf16[256,2048]{1,0:T(8,128)(2,1)} %get-tuple-element.154), channel_id=1, source_target_pairs={{0,120},{2,122},{4,124},{6,126},{8,0},{10,2},{12,4},{14,6},{16,8},... | collective-permute-start | bytes 3145736 | tf_op jit(solution)/shard_map/ppermute | solution.py:158
  9.9 4.1 %copy-start.1 = (bf16[1024,2048]{1,0:T(8,128)(2,1)S(1)}, bf16[1024,2048]{1,0:T(8,128)(2,1)}, u32[]{:S(2)}) copy-start(bf16[1024,2048]{1,0:T(8,128)(2,1)} %refs_0_.2) | copy-start | bytes 12582916
  18.0 25.7 %copy-start.3 = (s32[1,4]{1,0:T(1,128)S(1)}, s32[1,4]{1,0:T(1,128)}, u32[]{:S(2)}) copy-start(s32[1,4]{1,0:T(1,128)} %param.3) | copy-start | bytes 52
  32.1 12.7 %collective-permute-start.4 = (f32[512,1024]{1,0:T(8,128)}, f32[512,1024]{1,0:T(8,128)}, u32[]{:S(2)}, u32[]{:S(2)}) collective-permute-start(f32[512,1024]{1,0:T(8,128)} %shard_map.28), channel_id=1, source_target_pairs={{0,1},{1,0},{2,3},{3,2},{4,5},{5,4},{6,7},{7,6},{8,9},{9,8},{10,11... | collective-permute-start | bytes 6291464 | tf_op jit(solution)/shard_map/ppermute | solution.py:160
  33.6 11.2 %copy-start = (bf16[512,2048]{1,0:T(8,128)(2,1)S(1)}, bf16[512,2048]{1,0:T(8,128)(2,1)}, u32[]{:S(2)}) copy-start(bf16[512,2048]{1,0:T(8,128)(2,1)} %get-tuple-element.133.kept_ref) | copy-start | bytes 6291460
  33.6 11.2 %copy-start.2 = (bf16[1024,2048]{1,0:T(8,128)(2,1)S(1)}, bf16[1024,2048]{1,0:T(8,128)(2,1)}, u32[]{:S(2)}) copy-start(bf16[1024,2048]{1,0:T(8,128)(2,1)} %refs_0_.2) | copy-start | bytes 12582916
  35.5 25.4 %collective-permute-start.1 = (bf16[256,2048]{1,0:T(8,128)(2,1)S(1)}, bf16[256,2048]{1,0:T(8,128)(2,1)S(1)}, u32[]{:S(2)}, u32[]{:S(2)}) collective-permute-start(bf16[256,2048]{1,0:T(8,128)(2,1)S(1)} %get-tuple-element.148), channel_id=1, source_target_pairs={{0,6},{2,0},{4,2},{6,4},{8,14},{10,8},{12,10},{14,12},{16,22},{18,... | collective-permute-start | bytes 3145736 | tf_op jit(solution)/shard_map/ppermute | solution.py:158
  38.3 25.7 %collective-permute-start.2 = (bf16[256,2048]{1,0:T(8,128)(2,1)S(1)}, bf16[256,2048]{1,0:T(8,128)(2,1)S(1)}, u32[]{:S(2)}, u32[]{:S(2)}) collective-permute-start(bf16[256,2048]{1,0:T(8,128)(2,1)S(1)} %get-tuple-element.147), channel_id=1, source_target_pairs={{0,2},{2,4},{4,6},{6,0},{8,10},{10,12},{12,14},{14,8},{16,18},{18,... | collective-permute-start | bytes 3145736 | tf_op jit(solution)/shard_map/ppermute | solution.py:158
  38.3 28.0 %collective-permute-start.3 = (bf16[256,2048]{1,0:T(8,128)(2,1)}, bf16[256,2048]{1,0:T(8,128)(2,1)S(1)}, u32[]{:S(2)}, u32[]{:S(2)}) collective-permute-start(bf16[256,2048]{1,0:T(8,128)(2,1)} %get-tuple-element.75), channel_id=1, source_target_pairs={{0,120},{2,122},{4,124},{6,126},{8,0},{10,2},{12,4},{14,6},{16,8},... | collective-permute-start | bytes 3145736 | tf_op jit(solution)/shard_map/ppermute | solution.py:158
  66.6 23.6 %collective-permute-start.5 = (bf16[256,2048]{1,0:T(8,128)(2,1)S(1)}, bf16[256,2048]{1,0:T(8,128)(2,1)S(1)}, u32[]{:S(2)}, u32[]{:S(2)}) collective-permute-start(bf16[256,2048]{1,0:T(8,128)(2,1)S(1)} %get-tuple-element.146), channel_id=1, source_target_pairs={{0,6},{2,0},{4,2},{6,4},{8,14},{10,8},{12,10},{14,12},{16,22},{18,... | collective-permute-start | bytes 3145736 | tf_op jit(solution)/shard_map/ppermute | solution.py:158
  69.0 24.2 %collective-permute-start.6 = (bf16[256,2048]{1,0:T(8,128)(2,1)S(1)}, bf16[256,2048]{1,0:T(8,128)(2,1)S(1)}, u32[]{:S(2)}, u32[]{:S(2)}) collective-permute-start(bf16[256,2048]{1,0:T(8,128)(2,1)S(1)} %get-tuple-element.145), channel_id=1, source_target_pairs={{0,2},{2,4},{4,6},{6,0},{8,10},{10,12},{12,14},{14,8},{16,18},{18,... | collective-permute-start | bytes 3145736 | tf_op jit(solution)/shard_map/ppermute | solution.py:158
  69.0 26.2 %collective-permute-start.7 = (bf16[256,2048]{1,0:T(8,128)(2,1)S(1)}, bf16[256,2048]{1,0:T(8,128)(2,1)S(1)}, u32[]{:S(2)}, u32[]{:S(2)}) collective-permute-start(bf16[256,2048]{1,0:T(8,128)(2,1)S(1)} %get-tuple-element.84), channel_id=1, source_target_pairs={{0,120},{2,122},{4,124},{6,126},{8,0},{10,2},{12,4},{14,6},{16,8},... | collective-permute-start | bytes 3145736 | tf_op jit(solution)/shard_map/ppermute | solution.py:158
  74.4 4.0 %collective-permute-start.8 = (f32[512,256]{1,0:T(8,128)S(1)}, f32[512,256]{1,0:T(8,128)S(1)}, u32[]{:S(2)}, u32[]{:S(2)}) collective-permute-start(f32[512,256]{1,0:T(8,128)S(1)} %shard_map.29), channel_id=1, source_target_pairs={{0,1},{1,0},{2,3},{3,2},{4,5},{5,4},{6,7},{7,6},{8,9},{9,8},{10,11... | collective-permute-start | bytes 1572872 | tf_op jit(solution)/shard_map/ppermute | solution.py:160
  95.2 13.1 %collective-permute-start.12 = (f32[512,768]{1,0:T(8,128)S(1)}, f32[512,768]{1,0:T(8,128)S(1)}, u32[]{:S(2)}, u32[]{:S(2)}) collective-permute-start(f32[512,768]{1,0:T(8,128)S(1)} %shard_map.31), channel_id=1, source_target_pairs={{0,1},{1,0},{2,3},{3,2},{4,5},{5,4},{6,7},{7,6},{8,9},{9,8},{10,11... | collective-permute-start | bytes 4718600 | tf_op jit(solution)/shard_map/ppermute | solution.py:160
  97.9 26.1 %collective-permute-start.10 = (bf16[256,2048]{1,0:T(8,128)(2,1)S(1)}, bf16[256,2048]{1,0:T(8,128)(2,1)S(1)}, u32[]{:S(2)}, u32[]{:S(2)}) collective-permute-start(bf16[256,2048]{1,0:T(8,128)(2,1)S(1)} %get-tuple-element.143), channel_id=1, source_target_pairs={{0,2},{2,4},{4,6},{6,0},{8,10},{10,12},{12,14},{14,8},{16,18},{18,... | collective-permute-start | bytes 3145736 | tf_op jit(solution)/shard_map/ppermute | solution.py:158
  98.0 26.0 %collective-permute-start.9 = (bf16[256,2048]{1,0:T(8,128)(2,1)S(1)}, bf16[256,2048]{1,0:T(8,128)(2,1)S(1)}, u32[]{:S(2)}, u32[]{:S(2)}) collective-permute-start(bf16[256,2048]{1,0:T(8,128)(2,1)S(1)} %get-tuple-element.144), channel_id=1, source_target_pairs={{0,6},{2,0},{4,2},{6,4},{8,14},{10,8},{12,10},{14,12},{16,22},{18,... | collective-permute-start | bytes 3145736 | tf_op jit(solution)/shard_map/ppermute | solution.py:158
  100.7 27.6 %collective-permute-start.11 = (bf16[256,2048]{1,0:T(8,128)(2,1)S(1)}, bf16[256,2048]{1,0:T(8,128)(2,1)S(1)}, u32[]{:S(2)}, u32[]{:S(2)}) collective-permute-start(bf16[256,2048]{1,0:T(8,128)(2,1)S(1)} %get-tuple-element.96), channel_id=1, source_target_pairs={{0,120},{2,122},{4,124},{6,126},{8,0},{10,2},{12,4},{14,6},{16,8},... | collective-permute-start | bytes 3145736 | tf_op jit(solution)/shard_map/ppermute | solution.py:158
  128.3 5.0 %collective-permute-start.15 = (f32[512,768]{1,0:T(8,128)S(1)}, f32[512,768]{1,0:T(8,128)S(1)}, u32[]{:S(2)}, u32[]{:S(2)}) collective-permute-start(f32[512,768]{1,0:T(8,128)S(1)} %shard_map.33), channel_id=1, source_target_pairs={{0,1},{1,0},{2,3},{3,2},{4,5},{5,4},{6,7},{7,6},{8,9},{9,8},{10,11... | collective-permute-start | bytes 4718600 | tf_op jit(solution)/shard_map/ppermute | solution.py:160
  129.8 24.9 %collective-permute-start.13 = (bf16[256,2048]{1,0:T(8,128)(2,1)S(1)}, bf16[256,2048]{1,0:T(8,128)(2,1)S(1)}, u32[]{:S(2)}, u32[]{:S(2)}) collective-permute-start(bf16[256,2048]{1,0:T(8,128)(2,1)S(1)} %get-tuple-element.142), channel_id=1, source_target_pairs={{0,6},{2,0},{4,2},{6,4},{8,14},{10,8},{12,10},{14,12},{16,22},{18,... | collective-permute-start | bytes 3145736 | tf_op jit(solution)/shard_map/ppermute | solution.py:158
  131.2 25.7 %collective-permute-start.14 = (bf16[256,2048]{1,0:T(8,128)(2,1)S(1)}, bf16[256,2048]{1,0:T(8,128)(2,1)S(1)}, u32[]{:S(2)}, u32[]{:S(2)}) collective-permute-start(bf16[256,2048]{1,0:T(8,128)(2,1)S(1)} %get-tuple-element.141), channel_id=1, source_target_pairs={{0,2},{2,4},{4,6},{6,0},{8,10},{10,12},{12,14},{14,8},{16,18},{18,... | collective-permute-start | bytes 3145736 | tf_op jit(solution)/shard_map/ppermute | solution.py:158
  156.9 9.5 %collective-permute-start.18 = (f32[512,768]{1,0:T(8,128)S(1)}, f32[512,768]{1,0:T(8,128)S(1)}, u32[]{:S(2)}, u32[]{:S(2)}) collective-permute-start(f32[512,768]{1,0:T(8,128)S(1)} %shard_map.35), channel_id=1, source_target_pairs={{0,1},{1,0},{2,3},{3,2},{4,5},{5,4},{6,7},{7,6},{8,9},{9,8},{10,11... | collective-permute-start | bytes 4718600 | tf_op jit(solution)/shard_map/ppermute | solution.py:160
  158.0 30.2 %collective-permute-start.16 = (bf16[256,2048]{1,0:T(8,128)(2,1)S(1)}, bf16[256,2048]{1,0:T(8,128)(2,1)S(1)}, u32[]{:S(2)}, u32[]{:S(2)}) collective-permute-start(bf16[256,2048]{1,0:T(8,128)(2,1)S(1)} %collective-permute-done.2.refs_2_), channel_id=1, source_target_pairs={{0,2},{2,4},{4,6},{6,8},{8,10},{10,12},{12,14},{14,16},{16,18},{18... | collective-permute-start | bytes 3145736 | tf_op jit(solution)/shard_map/ppermute | solution.py:158
  158.0 30.2 %collective-permute-start.17 = (bf16[256,2048]{1,0:T(8,128)(2,1)S(1)}, bf16[256,2048]{1,0:T(8,128)(2,1)S(1)}, u32[]{:S(2)}, u32[]{:S(2)}) collective-permute-start(bf16[256,2048]{1,0:T(8,128)(2,1)S(1)} %collective-permute-done.9.refs_1_), channel_id=1, source_target_pairs={{0,126},{2,0},{4,2},{6,4},{8,6},{10,8},{12,10},{14,12},{16,14},{18... | collective-permute-start | bytes 3145736 | tf_op jit(solution)/shard_map/ppermute | solution.py:158
  188.2 9.2 %collective-permute-start.21 = (f32[512,512]{1,0:T(8,128)S(1)}, f32[512,512]{1,0:T(8,128)S(1)}, u32[]{:S(2)}, u32[]{:S(2)}) collective-permute-start(f32[512,512]{1,0:T(8,128)S(1)} %shard_map.37), channel_id=1, source_target_pairs={{0,1},{1,0},{2,3},{3,2},{4,5},{5,4},{6,7},{7,6},{8,9},{9,8},{10,11... | collective-permute-start | bytes 3145736 | tf_op jit(solution)/shard_map/ppermute | solution.py:160
  189.0 30.2 %collective-permute-start.19 = (bf16[256,2048]{1,0:T(8,128)(2,1)S(1)}, bf16[256,2048]{1,0:T(8,128)(2,1)S(1)}, u32[]{:S(2)}, u32[]{:S(2)}) collective-permute-start(bf16[256,2048]{1,0:T(8,128)(2,1)S(1)} %collective-permute-done.6.refs_2_), channel_id=1, source_target_pairs={{0,2},{2,4},{4,6},{6,8},{8,10},{10,12},{12,14},{14,16},{16,18},{18... | collective-permute-start | bytes 3145736 | tf_op jit(solution)/shard_map/ppermute | solution.py:158
  189.0 30.2 %collective-permute-start.20 = (bf16[256,2048]{1,0:T(8,128)(2,1)S(1)}, bf16[256,2048]{1,0:T(8,128)(2,1)S(1)}, u32[]{:S(2)}, u32[]{:S(2)}) collective-permute-start(bf16[256,2048]{1,0:T(8,128)(2,1)S(1)} %collective-permute-done.13.refs_0_), channel_id=1, source_target_pairs={{0,126},{2,0},{4,2},{6,4},{8,6},{10,8},{12,10},{14,12},{16,14},{18... | collective-permute-start | bytes 3145736 | tf_op jit(solution)/shard_map/ppermute | solution.py:158
  219.3 3.1 %collective-permute-start.23 = (f32[512,512]{1,0:T(8,128)S(1)}, f32[512,512]{1,0:T(8,128)S(1)}, u32[]{:S(2)}, u32[]{:S(2)}) collective-permute-start(f32[512,512]{1,0:T(8,128)S(1)} %shard_map.39), channel_id=1, source_target_pairs={{0,1},{1,0},{2,3},{3,2},{4,5},{5,4},{6,7},{7,6},{8,9},{9,8},{10,11... | collective-permute-start | bytes 3145736 | tf_op jit(solution)/shard_map/ppermute | solution.py:160
  221.5 4.1 %collective-permute-start.22 = (f32[512,512]{1,0:T(8,128)S(1)}, f32[512,512]{1,0:T(8,128)S(1)}, u32[]{:S(2)}, u32[]{:S(2)}) collective-permute-start(f32[512,512]{1,0:T(8,128)S(1)} %shard_map.41), channel_id=1, source_target_pairs={{0,1},{1,0},{2,3},{3,2},{4,5},{5,4},{6,7},{7,6},{8,9},{9,8},{10,11... | collective-permute-start | bytes 3145736 | tf_op jit(solution)/shard_map/ppermute | solution.py:174

commit v2 on v0

v2 whole, which is shorter than its diff:
```python
import jax
import jax.numpy as jnp
from jax import lax
from jax.experimental import pallas as pl
from jax.experimental.pallas import tpu as pltpu
from jax.sharding import PartitionSpec as P

RING = 4
STRIP = 256
MIB = 1 << 20
SMALL = pl.CostEstimate(flops=1, bytes_accessed=1, transcendentals=0)
VMEM = pl.BlockSpec(memory_space=pltpu.VMEM)
SMEM = pl.BlockSpec(memory_space=pltpu.SMEM)
ANY = pl.BlockSpec(memory_space=pl.ANY)
LIMIT = pltpu.CompilerParams(vmem_limit_bytes=28 * MIB)


def product(rows, partner):
    return lax.dot_general(
        rows, partner, (((1,), (1,)), ((), ())), preferred_element_type=jnp.float32
    )


def strips(height, run):
    @pl.loop(0, height // STRIP)
    def _(strip):
        run(pl.ds(pl.multiple_of(strip * STRIP, STRIP), STRIP))


def columns(group):
    first = 0
    for k, start, count in group:
        yield (k, start, count), pl.ds(first, count)
        first += count


def width(group):
    return sum(count for _, _, count in group)


def handed_products(handed, partners, group):
    height, arrays = handed.shape[0], list({id(p): p for p, _ in partners}.values())
    which = [[p is array for array in arrays].index(True) for p, _ in partners]

    def kernel(handed_ref, *refs):
        *array_refs, made_ref = refs
        for ((_, _, count), across), (_, start), at_array in zip(columns(group), partners, which):
            def strip(at):
                partner = array_refs[at_array][start:start + count, :]
                made_ref[at, across] = product(handed_ref[at, :], partner)
            strips(height, strip)

    return pl.pallas_call(
        kernel,
        out_shape=jax.ShapeDtypeStruct((height, width(group)), jnp.float32),
        in_specs=[VMEM] * (1 + len(arrays)),
        out_specs=VMEM,
        compiler_params=LIMIT,
        cost_estimate=SMALL,
    )(handed, *arrays)


def kept_products(out, weights, kept, theirs, partners, group, shape):
    height, arrays = kept.shape[0], list({id(p): p for p, _ in partners}.values())
    which = [[p is array for array in arrays].index(True) for p, _ in partners]
    first_call = out is None

    def kernel(weights_ref, kept_ref, theirs_ref, *refs):
        array_refs, refs = refs[:len(arrays)], refs[len(arrays):]
        out_ref, made_ref, sems = refs if first_call else refs[1:]
        copies = []
        for ((k, first, count), across), (_, start), at_array in zip(columns(group), partners, which):
            def strip(at):
                partner = array_refs[at_array][start:start + count, :]
                total = product(kept_ref[at, :], partner) + theirs_ref[at, across]
                made_ref[at, across] = total * weights_ref[k]
            strips(height, strip)
            copy = pltpu.make_async_copy(
                made_ref.at[:, across],
                out_ref.at[k, :, pl.ds(first, count)],
                sems.at[len(copies)],
            )
            copy.start()
            copies.append(copy)
        for copy in copies:
            copy.wait()

    return pl.pallas_call(
        kernel,
        out_shape=jax.ShapeDtypeStruct(shape, jnp.float32),
        in_specs=[SMEM] + [VMEM] * (2 + len(arrays)) + [ANY] * (not first_call),
        out_specs=ANY,
        scratch_shapes=[
            pltpu.VMEM((height, width(group)), jnp.float32),
            pltpu.SemaphoreType.DMA((len(group),)),
        ],
        input_output_aliases={} if first_call else {3 + len(arrays): 0},
        compiler_params=LIMIT,
        cost_estimate=SMALL,
    )(weights, kept, theirs, *arrays, *([] if first_call else [out]))


def relayed_products(where, rows, partners, theirs=()):
    size, many, sums = rows[0].shape[0], len(rows) // 2, len(theirs) > 0
    counts = [p.shape[0] - start for p, start in partners]

    def kernel(where_ref, *refs):
        row_refs, refs = refs[:len(rows)], refs[len(rows):]
        partner_refs, refs = refs[:len(partners)], refs[len(partners):]
        lower, upper = row_refs[:many], row_refs[many:]

        def run(chosen):
            for index, row_ref in enumerate(chosen):
                at, first = pl.ds(index * size, size), 0
                for n, (partner_ref, (_, start)) in enumerate(zip(partner_refs, partners)):
                    made = product(row_ref[...], partner_ref[start:, :])
                    if sums:
                        refs[-1][at, pl.ds(first, counts[n])] = made + refs[n][at, :]
                    else:
                        refs[n][at, :] = made
                    first += counts[n]

        pl.when(where_ref[0] == 0)(lambda: run(lower if sums else upper))
        pl.when(where_ref[0] == 1)(lambda: run(upper if sums else lower))

    widths = [sum(counts)] if sums else counts
    operands = [*rows, *(p for p, _ in partners), *theirs]
    return pl.pallas_call(
        kernel,
        out_shape=[jax.ShapeDtypeStruct((many * size, w), jnp.float32) for w in widths],
        in_specs=[SMEM] + [VMEM] * len(operands),
        out_specs=[VMEM] * len(widths),
        compiler_params=LIMIT,
        cost_estimate=SMALL,
    )(where, *operands)


def scaled_write(out, weights, made, tile, shape):
    k, first, count = tile

    def kernel(weights_ref, summed_ref, _, out_ref, made_ref, sem):
        def strip(at):
            made_ref[at, :] = summed_ref[at, :] * weights_ref[k]

        strips(made.shape[0], strip)
        copy = pltpu.make_async_copy(made_ref, out_ref.at[k, :, pl.ds(first, count)], sem)
        copy.start()
        copy.wait()

    return pl.pallas_call(
        kernel,
        out_shape=jax.ShapeDtypeStruct(shape, jnp.float32),
        in_specs=[SMEM, VMEM, ANY],
        out_specs=ANY,
        scratch_shapes=[pltpu.VMEM(made.shape, jnp.float32), pltpu.SemaphoreType.DMA],
        input_output_aliases={2: 0},
        compiler_params=LIMIT,
        cost_estimate=SMALL,
    )(weights, made, out)


def body(basis_rows, screen):
    blocks = lax.axis_size("blk")
    height = basis_rows.shape[0]
    half, q = height // 2, height // 4
    column = lax.axis_index("blk") % RING
    core = lax.axis_index("col")
    weights = jnp.concatenate([jnp.ones((1,), jnp.float32), screen[0].astype(jnp.float32)])
    where = core.astype(jnp.int32)[None]
    shape = (5, half, height)

    def below(distance):
        return [(i, (i - distance) % blocks) for i in range(blocks)]

    def around(distance):
        return [(i, i - i % RING + (i + distance) % RING) for i in range(blocks)]

    def swap(array):
        return lax.ppermute(array, "col", [(0, 1), (1, 0)])

    s = dict(own=basis_rows, held={}, made={}, out=None)

    def fence(*arrived):
        s["held"].update(arrived)
        s.update(lax.optimization_barrier(s))

    def mine(j):
        s["held"][0, j] = lax.slice_in_dim(s["own"], j * q, (j + 1) * q, axis=0)

    def fetch4(j):
        return (4, j), lax.ppermute(s["held"][0, j], "blk", below(4))

    def fetch1(j):
        send = jnp.where(column == 0, s["held"][4, j], s["held"][0, j])
        return (1, j), lax.ppermute(send, "blk", around(-1))

    def fetch3(j):
        send = jnp.where(column == RING - 1, s["held"][0, j], s["held"][4, j])
        return (3, j), lax.ppermute(send, "blk", around(1))

    def partners(group):
        found = []
        for k, first, _ in group:
            if k == 0:
                found.append((s["own"], first))
            elif k == 2:
                found.append((s["relayed"], first))
            else:
                found.append((s["held"][k, first // q], first % q))
        return found

    def make(*groups):
        for group in groups:
            s["made"][group] = handed_products(s["handed"], partners(group), group)

    def finish(*groups):
        for group in groups:
            theirs = swap(s["made"].pop(group))
            s["out"] = kept_products(
                s["out"], weights, s["kept"], theirs, partners(group), group, shape
            )

    e = q // 2
    own1, own2 = ((0, 0, 3 * e),), ((0, 3 * e, 3 * e),)
    own3 = ((0, 6 * e, q), (4, 0, e))
    four1 = ((4, e, e), (4, q, q))
    four2 = ((4, 2 * q, q), (1, 0, e))
    mixed1 = ((1, e, e), (3, 0, q))
    mixed2 = ((1, q, q), (3, q, e))
    four3 = ((4, 3 * q, q), (3, q + e, e))
    mixed3 = ((1, 2 * q, q), (3, 2 * q, q))
    mixed4 = ((1, 3 * q, q), (3, 3 * q, q))

    mine(0)
    fence()
    mine(1)
    s["kept"] = lax.dynamic_slice_in_dim(s["own"], core * half, half, 0)
    s["handed"] = lax.dynamic_slice_in_dim(s["own"], (1 - core) * half, half, 0)
    x0, x1 = fetch4(0), fetch4(1)
    make(own1)
    fence(x0)
    mine(2)
    d0, u0, x2 = fetch1(0), fetch3(0), fetch4(2)
    finish(own1)
    make(own2)
    fence(x1)
    mine(3)
    d1, u1 = fetch1(1), fetch3(1)
    fence(d0, u0)
    x3 = fetch4(3)
    finish(own2)
    make(own3, four1)
    fence(x2)
    d2, u2 = fetch1(2), fetch3(2)
    fence(d1, u1)
    finish(own3, four1)
    make(four2, mixed1, mixed2)
    fence(x3)
    d3, u3 = fetch1(3), fetch3(3)
    fence(d2, u2)
    finish(four2, mixed1, mixed2)
    make(four3, mixed3)
    relay = q + e
    s["relay"] = jnp.concatenate([s["held"][1, 0], s["held"][1, 1][:e]])
    fence(d3, u3)

    relayed = lax.ppermute(s["relay"], "blk", below(1))
    rows = [s["held"][1, j] for j in range(4)]
    others = [(s["held"][3, 1], e), (s["held"][3, 2], 0), (s["held"][3, 3], 0)]
    theirs = [swap(array) for array in relayed_products(where, rows, others)]
    s["ahead"], = relayed_products(where, rows, others, theirs)
    make(mixed4)
    fence()

    ahead = lax.ppermute(s["ahead"], "blk", below(-1))
    finish(four3, mixed3, mixed4)
    s["relayed"] = relayed
    fence()

    group = ((2, 0, relay),)
    make(group)
    finish(group)
    out = scaled_write(s["out"], weights, ahead, (2, relay, height - relay), shape)
    return out[None]


def solution(mesh):
    return jax.shard_map(
        body,
        mesh=mesh,
        in_specs=(P("blk", "col"), P("blk", None)),
        out_specs=P("blk", None, "col", None),
        check_vma=False,
    )
```

time: 907 us -> 187 us (0.21)
  waiting for transfers between devices: 842 us -> 67.7 us
  Pallas kernels: 0 us -> 60.1 us
  starting transfers between devices: 5.42 us -> 45 us
  matrix products: 34.4 us -> 0 us
  between operations: 13.4 us -> 0.57 us
  local copies, waits for them, and re-layouts: 0.63 us -> 9.9 us
    ppermute x4 -> x28, waiting for transfers between devices: 493 us -> 67.7 us  [the longest x4 19.7 us: fetch1(): return ((1, j), lax.ppermute(send, 'blk', around(-1)))]
    reduce_scatter x1 -> x0, waiting for transfers between devices: 349 us -> none  [body(): summed = lax.psum_scatter(terms, 'col', scatter_dimension=1, tiled=True)]
    pallas_call x0 -> x25, Pallas kernels: none -> 60.1 us  [the longest x11 34.6 us: kept_products(): pl.pallas_call(kernel, out_shape=jax.ShapeDtypeStruct(shape, jnp.float32)...]
    ppermute x4 -> x28, starting transfers between devices: 5.42 us -> 45 us  [the longest x4 18.2 us: fetch4(): return ((4, j), lax.ppermute(s['held'][0, j], 'blk', below(4)))]
    dot_general x5 -> x0, matrix products: 34.4 us -> none  [full_term(): lax.dot_general(own, partner, (((1,), (1,)), ((), ())), preferred_element...]
    broadcast_in_dim x1 -> x0, other arithmetic: 10.6 us -> none  [body(): return (summed * weights[:, None, None])[None]]
  transfers between devices with their start and end apart: 5 -> 28, of which waited for: 3 -> 13; matrix products, arithmetic and copies ran while one was open for 3% -> 5% of each run, Pallas kernels for 0% -> 30%
where the time goes in v2:
time: 187 us
  waiting for transfers between devices  67.7 us (36%)
  Pallas kernels  60.1 us (32%)
  starting transfers between devices  45 us (24%)
  local copies, waits for them, and re-layouts  9.9 us (5%)
  other arithmetic  3.57 us (2%)
    pallas_call x11, Pallas kernels, kept_products(): pl.pallas_call(kernel, out_shape=jax.ShapeDtypeStruct(shape, jnp.float32)...  34.6 us
    pallas_call x11, Pallas kernels, handed_products(): pl.pallas_call(kernel, out_shape=jax.ShapeDtypeStruct((height, width(grou...  20.2 us
    ppermute x4, waiting for transfers between devices, fetch1(): return ((1, j), lax.ppermute(send, 'blk', around(-1)))  19.7 us
    ppermute x4, waiting for transfers between devices, fetch4(): return ((4, j), lax.ppermute(s['held'][0, j], 'blk', below(4)))  18.4 us
    ppermute x4, starting transfers between devices, fetch4(): return ((4, j), lax.ppermute(s['held'][0, j], 'blk', below(4)))  18.2 us
    ppermute x1, waiting for transfers between devices, body(): relayed = lax.ppermute(s['relay'], 'blk', below(1))  14 us
    ppermute x14, starting transfers between devices, swap(): return lax.ppermute(array, 'col', [(0, 1), (1, 0)])  13.2 us
    ppermute x4, waiting for transfers between devices, fetch3(): return ((3, j), lax.ppermute(send, 'blk', around(1)))  9.13 us
  transfers between devices with their start and end apart: 28, of which 13 were waited for; matrix products, arithmetic and copies ran while one was open for 5% of the time, Pallas kernels for 30%

profile of v2, /device:TPU:1, one launch (start us, length us, event | category | flops | bytes accessed | tf_op | source)
XLA Modules:
  0.0 186.8 jit_solution(15730198950273883532)
XLA Ops:
  0.0 2.3 %slice.15 = bf16[256,2048]{1,0:T(8,128)(2,1)} slice(bf16[1024,2048]{1,0:T(8,128)(2,1)} %refs_0_.5), slice={[0:256], [0:2048]} | slice | bytes 2097152 | tf_op jit(solution)/shard_map/slice | solution.py:188
  2.3 6.8 %collective-permute-start = (bf16[256,2048]{1,0:T(8,128)(2,1)}, bf16[256,2048]{1,0:T(8,128)(2,1)S(1)}, u32[]{:S(2)}, u32[]{:S(2)}) collective-permute-start(bf16[256,2048]{1,0:T(8,128)(2,1)} %slice.15), channel_id=1, source_target_pairs={{0,120},{2,122},{4,124},{6,126},{8,0},{10,2},{12,4},{14,6},{16,8},... | collective-permute-start | bytes 3145736 | tf_op jit(solution)/shard_map/ppermute | solution.py:191
  12.0 4.1 %constant_dynamic-slice_fusion = (bf16[512,2048]{1,0:T(8,128)(2,1)}, bf16[512,2048]{1,0:T(8,128)(2,1)S(1)}) fusion(bf16[1024,2048]{1,0:T(8,128)(2,1)} %refs_0_.5, s32[]{:T(128)S(6)} %select_n.52, s32[]{:T(128)S(6)} %select_n.51), kind=kLoop, calls=%fused_computation.10 | loop fusion | bytes 8388616 | tf_op jit(solution)/shard_map/dynamic_slice | solution.py:237
  18.4 12.8 %collective-permute-done.refs_1_.refs_0_ = bf16[256,2048]{1,0:T(8,128)(2,1)S(1)} collective-permute-done((bf16[256,2048]{1,0:T(8,128)(2,1)}, bf16[256,2048]{1,0:T(8,128)(2,1)S(1)}, u32[]{:S(2)}, u32[]{:S(2)}) %collective-permute-start) | collective-permute-done | bytes 1048608 | tf_op jit(solution)/shard_map/ppermute | solution.py:191
  31.2 2.7 %collective-permute-start.2 = (f32[512,384]{1,0:T(8,128)}, f32[512,384]{1,0:T(8,128)S(1)}, u32[]{:S(2)}, u32[]{:S(2)}) collective-permute-start(f32[512,384]{1,0:T(8,128)} %copy-done.3), channel_id=1, source_target_pairs={{0,1},{1,0},{2,3},{3,2},{4,5},{5,4},{6,7},{7,6},{8,9},{9,8},{10,11... | collective-permute-start | bytes 2359304 | tf_op jit(solution)/shard_map/ppermute | solution.py:179
  35.3 2.8 %collective-permute-start.3 = (bf16[256,2048]{1,0:T(8,128)(2,1)S(1)}, bf16[256,2048]{1,0:T(8,128)(2,1)S(1)}, u32[]{:S(2)}, u32[]{:S(2)}) collective-permute-start(bf16[256,2048]{1,0:T(8,128)(2,1)S(1)} %get-tuple-element.248), channel_id=1, source_target_pairs={{0,6},{2,0},{4,2},{6,4},{8,14},{10,8},{12,10},{14,12},{16,22},{18,... | collective-permute-start | bytes 3145736 | tf_op jit(solution)/shard_map/ppermute | solution.py:195
  39.8 5.5 %collective-permute-start.5 = (bf16[256,2048]{1,0:T(8,128)(2,1)S(1)}, bf16[256,2048]{1,0:T(8,128)(2,1)S(1)}, u32[]{:S(2)}, u32[]{:S(2)}) collective-permute-start(bf16[256,2048]{1,0:T(8,128)(2,1)S(1)} %slice.17), channel_id=1, source_target_pairs={{0,120},{2,122},{4,124},{6,126},{8,0},{10,2},{12,4},{14,6},{16,8},... | collective-permute-start | bytes 3145736 | tf_op jit(solution)/shard_map/ppermute | solution.py:191
  45.2 2.9 %shard_map.30.refs_1_ = f32[5,512,1024]{2,1,0:T(8,128)} custom-call(f32[5]{0:T(128)S(1)} %pad_maximum_fusion.1.weights_ref, bf16[512,2048]{1,0:T(8,128)(2,1)S(1)} %copy-done, f32[512,384]{1,0:T(8,128)S(1)} %collective-permute-done.2.theirs_ref, bf16[1024,2048]{1,0:T(8,128)(2,1)S(1)} %copy-done.2), custom_call_target="tpu_custom_call" | custom-call | flops 1 | bytes 1 | tf_op jit(solution)/shard_map/pallas_call | solution.py:88
  48.1 5.6 %collective-permute-done.1.refs_1_ = bf16[256,2048]{1,0:T(8,128)(2,1)} collective-permute-done((bf16[256,2048]{1,0:T(8,128)(2,1)}, bf16[256,2048]{1,0:T(8,128)(2,1)}, u32[]{:S(2)}, u32[]{:S(2)}) %collective-permute-start.1) | collective-permute-done | bytes 1048608 | tf_op jit(solution)/shard_map/ppermute | solution.py:191
  55.4 2.8 %collective-permute-start.7 = (bf16[256,2048]{1,0:T(8,128)(2,1)S(1)}, bf16[256,2048]{1,0:T(8,128)(2,1)S(1)}, u32[]{:S(2)}, u32[]{:S(2)}) collective-permute-start(bf16[256,2048]{1,0:T(8,128)(2,1)S(1)} %get-tuple-element.246), channel_id=1, source_target_pairs={{0,6},{2,0},{4,2},{6,4},{8,14},{10,8},{12,10},{14,12},{16,22},{18,... | collective-permute-start | bytes 3145736 | tf_op jit(solution)/shard_map/ppermute | solution.py:195
  58.3 2.4 %collective-permute-done.3.refs_0_.refs_1_ = bf16[256,2048]{1,0:T(8,128)(2,1)S(1)} collective-permute-done((bf16[256,2048]{1,0:T(8,128)(2,1)S(1)}, bf16[256,2048]{1,0:T(8,128)(2,1)S(1)}, u32[]{:S(2)}, u32[]{:S(2)}) %collective-permute-start.3) | collective-permute-done | bytes 1048608 | tf_op jit(solution)/shard_map/ppermute | solution.py:195
  60.7 3.1 %collective-permute-done.4.refs_1_ = bf16[256,2048]{1,0:T(8,128)(2,1)S(1)} collective-permute-done((bf16[256,2048]{1,0:T(8,128)(2,1)S(1)}, bf16[256,2048]{1,0:T(8,128)(2,1)S(1)}, u32[]{:S(2)}, u32[]{:S(2)}) %collective-permute-start.4) | collective-permute-done | bytes 1048608 | tf_op jit(solution)/shard_map/ppermute | solution.py:199
  65.6 5.4 %collective-permute-start.9 = (bf16[256,2048]{1,0:T(8,128)(2,1)S(1)}, bf16[256,2048]{1,0:T(8,128)(2,1)S(1)}, u32[]{:S(2)}, u32[]{:S(2)}) collective-permute-start(bf16[256,2048]{1,0:T(8,128)(2,1)S(1)} %slice.18), channel_id=1, source_target_pairs={{0,120},{2,122},{4,124},{6,126},{8,0},{10,2},{12,4},{14,6},{16,8},... | collective-permute-start | bytes 3145736 | tf_op jit(solution)/shard_map/ppermute | solution.py:191
  71.0 3.0 %shard_map.32 = f32[512,384]{1,0:T(8,128)S(1)} custom-call(bf16[512,2048]{1,0:T(8,128)(2,1)S(1)} %get-tuple-element.236.handed_ref, bf16[256,2048]{1,0:T(8,128)(2,1)S(1)} %collective-permute-done.refs_1_.refs_0_, bf16[256,2048]{1,0:T(8,128)(2,1)} %collective-permute-done.1.refs_1_), custom_call_target="tpu_custom_call" | custom-call | flops 1 | bytes 1 | tf_op jit(solution)/shard_map/pallas_call | solution.py:53
  75.9 2.9 %shard_map.33.refs_2_ = f32[5,512,1024]{2,1,0:T(8,128)} custom-call(f32[5]{0:T(128)S(1)} %pad_maximum_fusion.1.weights_ref, bf16[512,2048]{1,0:T(8,128)(2,1)S(1)} %copy-done, f32[512,384]{1,0:T(8,128)S(1)} %collective-permute-done.6.theirs_ref, bf16[1024,2048]{1,0:T(8,128)(2,1)S(1)} %copy-done.2, ...), custom_call_target="tpu_custom_call", output_to_operand_aliasing={{}: (4, {})} | custom-call | flops 1 | bytes 1 | tf_op jit(solution)/shard_map/pallas_call | solution.py:88
  78.8 3.9 %collective-permute-done.7.refs_0_.refs_1_ = bf16[256,2048]{1,0:T(8,128)(2,1)S(1)} collective-permute-done((bf16[256,2048]{1,0:T(8,128)(2,1)S(1)}, bf16[256,2048]{1,0:T(8,128)(2,1)S(1)}, u32[]{:S(2)}, u32[]{:S(2)}) %collective-permute-start.7) | collective-permute-done | bytes 1048608 | tf_op jit(solution)/shard_map/ppermute | solution.py:195
  82.7 3.1 %collective-permute-done.8.refs_1_.refs_4_ = bf16[256,2048]{1,0:T(8,128)(2,1)S(1)} collective-permute-done((bf16[256,2048]{1,0:T(8,128)(2,1)S(1)}, bf16[256,2048]{1,0:T(8,128)(2,1)S(1)}, u32[]{:S(2)}, u32[]{:S(2)}) %collective-permute-start.8) | collective-permute-done | bytes 1048608 | tf_op jit(solution)/shard_map/ppermute | solution.py:199
  94.5 3.1 %shard_map.37.refs_2_ = f32[5,512,1024]{2,1,0:T(8,128)} custom-call(f32[5]{0:T(128)S(1)} %pad_maximum_fusion.1.weights_ref, bf16[512,2048]{1,0:T(8,128)(2,1)S(1)} %copy-done, f32[512,384]{1,0:T(8,128)S(1)} %collective-permute-done.11.theirs_ref, bf16[1024,2048]{1,0:T(8,128)(2,1)S(1)} %copy-done.2, ...), custom_call_target="tpu_custom_call", output_to_operand_aliasing={{}: (5, {})} | custom-call | flops 1 | bytes 1 | tf_op jit(solution)/shard_map/pallas_call | solution.py:88
  97.6 3.9 %shard_map.38.refs_2_ = f32[5,512,1024]{2,1,0:T(8,128)} custom-call(f32[5]{0:T(128)S(1)} %pad_maximum_fusion.1.weights_ref, bf16[512,2048]{1,0:T(8,128)(2,1)S(1)} %copy-done, f32[512,384]{1,0:T(8,128)S(1)} %collective-permute-done.10.theirs_ref, bf16[256,2048]{1,0:T(8,128)(2,1)S(1)} %collective-permute-done.refs_1_.refs_0_, ...), custom_call_target="tpu_custom_call", output_to_operand_aliasing={{}: (5, {})} | custom-call | flops 1 | bytes 1 | tf_op jit(solution)/shard_map/pallas_call | solution.py:88
  103.2 8.5 %collective-permute-done.12.refs_0_.refs_2_ = bf16[256,2048]{1,0:T(8,128)(2,1)S(1)} collective-permute-done((bf16[256,2048]{1,0:T(8,128)(2,1)S(1)}, bf16[256,2048]{1,0:T(8,128)(2,1)S(1)}, u32[]{:S(2)}, u32[]{:S(2)}) %collective-permute-start.12) | collective-permute-done | bytes 1048608 | tf_op jit(solution)/shard_map/ppermute | solution.py:195
  113.2 2.4 %collective-permute-start.18 = (f32[512,384]{1,0:T(8,128)S(1)}, f32[512,384]{1,0:T(8,128)S(1)}, u32[]{:S(2)}, u32[]{:S(2)}) collective-permute-start(f32[512,384]{1,0:T(8,128)S(1)} %shard_map.36), channel_id=1, source_target_pairs={{0,1},{1,0},{2,3},{3,2},{4,5},{5,4},{6,7},{7,6},{8,9},{9,8},{10,11... | collective-permute-start | bytes 2359304 | tf_op jit(solution)/shard_map/ppermute | solution.py:179
  120.1 3.1 %shard_map.41.refs_2_ = f32[5,512,1024]{2,1,0:T(8,128)} custom-call(f32[5]{0:T(128)S(1)} %pad_maximum_fusion.1.weights_ref, bf16[512,2048]{1,0:T(8,128)(2,1)S(1)} %copy-done, f32[512,384]{1,0:T(8,128)S(1)} %collective-permute-done.18.theirs_ref, bf16[256,2048]{1,0:T(8,128)(2,1)S(1)} %collective-permute-done.5.refs_0_, ...), custom_call_target="tpu_custom_call", output_to_operand_aliasing={{}: (5, {})} | custom-call | flops 1 | bytes 1 | tf_op jit(solution)/shard_map/pallas_call | solution.py:88
  123.2 3.2 %shard_map.42.refs_2_ = f32[5,512,1024]{2,1,0:T(8,128)} custom-call(f32[5]{0:T(128)S(1)} %pad_maximum_fusion.1.weights_ref, bf16[512,2048]{1,0:T(8,128)(2,1)S(1)} %copy-done, f32[512,384]{1,0:T(8,128)S(1)} %collective-permute-done.17.theirs_ref, bf16[256,2048]{1,0:T(8,128)(2,1)S(1)} %collective-permute-done.3.refs_0_.refs_1_, ...), custom_call_target="tpu_custom_call", output_to_operand_aliasing={{}: (5, {})} | custom-call | flops 1 | bytes 1 | tf_op jit(solution)/shard_map/pallas_call | solution.py:88
  126.4 3.1 %shard_map.43.refs_2_ = f32[5,512,1024]{2,1,0:T(8,128)} custom-call(f32[5]{0:T(128)S(1)} %pad_maximum_fusion.1.weights_ref, bf16[512,2048]{1,0:T(8,128)(2,1)S(1)} %copy-done, f32[512,384]{1,0:T(8,128)S(1)} %collective-permute-done.16.theirs_ref, bf16[256,2048]{1,0:T(8,128)(2,1)S(1)} %collective-permute-done.7.refs_0_.refs_1_, ...), custom_call_target="tpu_custom_call", output_to_operand_aliasing={{}: (5, {})} | custom-call | flops 1 | bytes 1 | tf_op jit(solution)/shard_map/pallas_call | solution.py:88
  129.4 4.8 %collective-permute-done.14.refs_3_.refs_0_ = bf16[256,2048]{1,0:T(8,128)(2,1)S(1)} collective-permute-done((bf16[256,2048]{1,0:T(8,128)(2,1)S(1)}, bf16[256,2048]{1,0:T(8,128)(2,1)S(1)}, u32[]{:S(2)}, u32[]{:S(2)}) %collective-permute-start.14) | collective-permute-done | bytes 1048608 | tf_op jit(solution)/shard_map/ppermute | solution.py:195
  139.1 4.9 %collective-permute-start.26 = (bf16[384,2048]{1,0:T(8,128)(2,1)S(1)}, bf16[384,2048]{1,0:T(8,128)(2,1)S(1)}, u32[]{:S(2)}, u32[]{:S(2)}) collective-permute-start(bf16[384,2048]{1,0:T(8,128)(2,1)S(1)} %pad_maximum_fusion), channel_id=1, source_target_pairs={{0,126},{2,0},{4,2},{6,4},{8,6},{10,8},{12,10},{14,12},{16,14},{18... | collective-permute-start | bytes 4718600 | tf_op jit(solution)/shard_map/ppermute | solution.py:267
  149.1 4.7 %collective-permute-done.25.theirs_ref = f32[512,384]{1,0:T(8,128)S(1)} collective-permute-done((f32[512,384]{1,0:T(8,128)S(1)}, f32[512,384]{1,0:T(8,128)S(1)}, u32[]{:S(2)}, u32[]{:S(2)}) %collective-permute-start.25) | collective-permute-done | bytes 786464 | tf_op jit(solution)/shard_map/ppermute | solution.py:179
  153.7 3.1 %shard_map.47.refs_2_ = f32[5,512,1024]{2,1,0:T(8,128)} custom-call(f32[5]{0:T(128)S(1)} %pad_maximum_fusion.1.weights_ref, bf16[512,2048]{1,0:T(8,128)(2,1)S(1)} %copy-done, f32[512,384]{1,0:T(8,128)S(1)} %collective-permute-done.25.theirs_ref, bf16[256,2048]{1,0:T(8,128)(2,1)S(1)} %collective-permute-done.9.refs_0_, ...), custom_call_target="tpu_custom_call", output_to_operand_aliasing={{}: (5, {})} | custom-call | flops 1 | bytes 1 | tf_op jit(solution)/shard_map/pallas_call | solution.py:88
  156.8 3.2 %shard_map.48.refs_2_ = f32[5,512,1024]{2,1,0:T(8,128)} custom-call(f32[5]{0:T(128)S(1)} %pad_maximum_fusion.1.weights_ref, bf16[512,2048]{1,0:T(8,128)(2,1)S(1)} %copy-done, f32[512,512]{1,0:T(8,128)S(1)} %collective-permute-done.24.theirs_ref, bf16[256,2048]{1,0:T(8,128)(2,1)S(1)} %collective-permute-done.12.refs_0_.refs_2_, ...), custom_call_target="tpu_custom_call", output_to_operand_aliasing={{}: (5, {})} | custom-call | flops 1 | bytes 1 | tf_op jit(solution)/shard_map/pallas_call | solution.py:88
  160.1 3.2 %shard_map.49.refs_1_ = f32[5,512,1024]{2,1,0:T(8,128)} custom-call(f32[5]{0:T(128)S(1)} %pad_maximum_fusion.1.weights_ref, bf16[512,2048]{1,0:T(8,128)(2,1)S(1)} %copy-done, f32[512,512]{1,0:T(8,128)S(1)} %collective-permute-done.23.theirs_ref, bf16[256,2048]{1,0:T(8,128)(2,1)S(1)} %collective-permute-done.14.refs_3_.refs_0_, ...), custom_call_target="tpu_custom_call", output_to_operand_aliasing={{}: (5, {})} | custom-call | flops 1 | bytes 1 | tf_op jit(solution)/shard_map/pallas_call | solution.py:88
  163.3 14.0 %collective-permute-done.26.refs_0_ = bf16[384,2048]{1,0:T(8,128)(2,1)S(1)} collective-permute-done((bf16[384,2048]{1,0:T(8,128)(2,1)S(1)}, bf16[384,2048]{1,0:T(8,128)(2,1)S(1)}, u32[]{:S(2)}, u32[]{:S(2)}) %collective-permute-start.26) | collective-permute-done | bytes 1572896 | tf_op jit(solution)/shard_map/ppermute | solution.py:267
  182.0 2.9 %shard_map.51._ = f32[5,512,1024]{2,1,0:T(8,128)} custom-call(f32[5]{0:T(128)S(1)} %pad_maximum_fusion.1.weights_ref, bf16[512,2048]{1,0:T(8,128)(2,1)S(1)} %copy-done, f32[512,384]{1,0:T(8,128)S(1)} %collective-permute-done.27.theirs_ref, bf16[384,2048]{1,0:T(8,128)(2,1)S(1)} %collective-permute-done.26.refs_0_, ...), custom_call_target="tpu_custom_call", output_to_operand_aliasing={{}: (4, {})} | custom-call | flops 1 | bytes 1 | tf_op jit(solution)/shard_map/pallas_call | solution.py:88
  (72 shorter events, 46.0 us)
Async XLA Ops:
  2.3 28.9 %collective-permute-start = (bf16[256,2048]{1,0:T(8,128)(2,1)}, bf16[256,2048]{1,0:T(8,128)(2,1)S(1)}, u32[]{:S(2)}, u32[]{:S(2)}) collective-permute-start(bf16[256,2048]{1,0:T(8,128)(2,1)} %slice.15), channel_id=1, source_target_pairs={{0,120},{2,122},{4,124},{6,126},{8,0},{10,2},{12,4},{14,6},{16,8},... | collective-permute-start | bytes 3145736 | tf_op jit(solution)/shard_map/ppermute | solution.py:191
  11.4 42.3 %collective-permute-start.1 = (bf16[256,2048]{1,0:T(8,128)(2,1)}, bf16[256,2048]{1,0:T(8,128)(2,1)}, u32[]{:S(2)}, u32[]{:S(2)}) collective-permute-start(bf16[256,2048]{1,0:T(8,128)(2,1)} %slice.16), channel_id=1, source_target_pairs={{0,120},{2,122},{4,124},{6,126},{8,0},{10,2},{12,4},{14,6},{16,8},... | collective-permute-start | bytes 3145736 | tf_op jit(solution)/shard_map/ppermute | solution.py:191
  11.9 4.1 %copy-start.1 = (bf16[1024,2048]{1,0:T(8,128)(2,1)S(1)}, bf16[1024,2048]{1,0:T(8,128)(2,1)}, u32[]{:S(2)}) copy-start(bf16[1024,2048]{1,0:T(8,128)(2,1)} %refs_0_.5) | copy-start | bytes 12582916
  16.1 22.0 %copy-start.4 = (s32[1,4]{1,0:T(1,128)S(1)}, s32[1,4]{1,0:T(1,128)}, u32[]{:S(2)}) copy-start(s32[1,4]{1,0:T(1,128)} %param.3) | copy-start | bytes 52
  18.4 19.7 %copy-start.2 = (bf16[1024,2048]{1,0:T(8,128)(2,1)S(1)}, bf16[1024,2048]{1,0:T(8,128)(2,1)}, u32[]{:S(2)}) copy-start(bf16[1024,2048]{1,0:T(8,128)(2,1)} %refs_0_.5) | copy-start | bytes 12582916
  31.2 14.0 %collective-permute-start.2 = (f32[512,384]{1,0:T(8,128)}, f32[512,384]{1,0:T(8,128)S(1)}, u32[]{:S(2)}, u32[]{:S(2)}) collective-permute-start(f32[512,384]{1,0:T(8,128)} %copy-done.3), channel_id=1, source_target_pairs={{0,1},{1,0},{2,3},{3,2},{4,5},{5,4},{6,7},{7,6},{8,9},{9,8},{10,11... | collective-permute-start | bytes 2359304 | tf_op jit(solution)/shard_map/ppermute | solution.py:179
  35.3 25.4 %collective-permute-start.3 = (bf16[256,2048]{1,0:T(8,128)(2,1)S(1)}, bf16[256,2048]{1,0:T(8,128)(2,1)S(1)}, u32[]{:S(2)}, u32[]{:S(2)}) collective-permute-start(bf16[256,2048]{1,0:T(8,128)(2,1)S(1)} %get-tuple-element.248), channel_id=1, source_target_pairs={{0,6},{2,0},{4,2},{6,4},{8,14},{10,8},{12,10},{14,12},{16,22},{18,... | collective-permute-start | bytes 3145736 | tf_op jit(solution)/shard_map/ppermute | solution.py:195
  38.1 25.7 %collective-permute-start.4 = (bf16[256,2048]{1,0:T(8,128)(2,1)S(1)}, bf16[256,2048]{1,0:T(8,128)(2,1)S(1)}, u32[]{:S(2)}, u32[]{:S(2)}) collective-permute-start(bf16[256,2048]{1,0:T(8,128)(2,1)S(1)} %get-tuple-element.247), channel_id=1, source_target_pairs={{0,2},{2,4},{4,6},{6,0},{8,10},{10,12},{12,14},{14,8},{16,18},{18,... | collective-permute-start | bytes 3145736 | tf_op jit(solution)/shard_map/ppermute | solution.py:199
  38.2 7.1 %copy-start = (bf16[512,2048]{1,0:T(8,128)(2,1)S(1)}, bf16[512,2048]{1,0:T(8,128)(2,1)}, u32[]{:S(2)}) copy-start(bf16[512,2048]{1,0:T(8,128)(2,1)} %get-tuple-element.235.kept_ref) | copy-start | bytes 6291460
  39.8 39.0 %collective-permute-start.5 = (bf16[256,2048]{1,0:T(8,128)(2,1)S(1)}, bf16[256,2048]{1,0:T(8,128)(2,1)S(1)}, u32[]{:S(2)}, u32[]{:S(2)}) collective-permute-start(bf16[256,2048]{1,0:T(8,128)(2,1)S(1)} %slice.17), channel_id=1, source_target_pairs={{0,120},{2,122},{4,124},{6,126},{8,0},{10,2},{12,4},{14,6},{16,8},... | collective-permute-start | bytes 3145736 | tf_op jit(solution)/shard_map/ppermute | solution.py:191
  55.4 27.3 %collective-permute-start.7 = (bf16[256,2048]{1,0:T(8,128)(2,1)S(1)}, bf16[256,2048]{1,0:T(8,128)(2,1)S(1)}, u32[]{:S(2)}, u32[]{:S(2)}) collective-permute-start(bf16[256,2048]{1,0:T(8,128)(2,1)S(1)} %get-tuple-element.246), channel_id=1, source_target_pairs={{0,6},{2,0},{4,2},{6,4},{8,14},{10,8},{12,10},{14,12},{16,22},{18,... | collective-permute-start | bytes 3145736 | tf_op jit(solution)/shard_map/ppermute | solution.py:195
  58.2 27.6 %collective-permute-start.8 = (bf16[256,2048]{1,0:T(8,128)(2,1)S(1)}, bf16[256,2048]{1,0:T(8,128)(2,1)S(1)}, u32[]{:S(2)}, u32[]{:S(2)}) collective-permute-start(bf16[256,2048]{1,0:T(8,128)(2,1)S(1)} %get-tuple-element.245), channel_id=1, source_target_pairs={{0,2},{2,4},{4,6},{6,0},{8,10},{10,12},{12,14},{14,8},{16,18},{18,... | collective-permute-start | bytes 3145736 | tf_op jit(solution)/shard_map/ppermute | solution.py:199
  63.8 12.1 %collective-permute-start.6 = (f32[512,384]{1,0:T(8,128)S(1)}, f32[512,384]{1,0:T(8,128)S(1)}, u32[]{:S(2)}, u32[]{:S(2)}) collective-permute-start(f32[512,384]{1,0:T(8,128)S(1)} %shard_map.29), channel_id=1, source_target_pairs={{0,1},{1,0},{2,3},{3,2},{4,5},{5,4},{6,7},{7,6},{8,9},{9,8},{10,11... | collective-permute-start | bytes 2359304 | tf_op jit(solution)/shard_map/ppermute | solution.py:179
  65.6 36.0 %collective-permute-start.9 = (bf16[256,2048]{1,0:T(8,128)(2,1)S(1)}, bf16[256,2048]{1,0:T(8,128)(2,1)S(1)}, u32[]{:S(2)}, u32[]{:S(2)}) collective-permute-start(bf16[256,2048]{1,0:T(8,128)(2,1)S(1)} %slice.18), channel_id=1, source_target_pairs={{0,120},{2,122},{4,124},{6,126},{8,0},{10,2},{12,4},{14,6},{16,8},... | collective-permute-start | bytes 3145736 | tf_op jit(solution)/shard_map/ppermute | solution.py:191
  85.8 8.6 %collective-permute-start.11 = (f32[512,384]{1,0:T(8,128)S(1)}, f32[512,384]{1,0:T(8,128)S(1)}, u32[]{:S(2)}, u32[]{:S(2)}) collective-permute-start(f32[512,384]{1,0:T(8,128)S(1)} %shard_map.31), channel_id=1, source_target_pairs={{0,1},{1,0},{2,3},{3,2},{4,5},{5,4},{6,7},{7,6},{8,9},{9,8},{10,11... | collective-permute-start | bytes 2359304 | tf_op jit(solution)/shard_map/ppermute | solution.py:179
  87.4 10.3 %collective-permute-start.10 = (f32[512,384]{1,0:T(8,128)S(1)}, f32[512,384]{1,0:T(8,128)S(1)}, u32[]{:S(2)}, u32[]{:S(2)}) collective-permute-start(f32[512,384]{1,0:T(8,128)S(1)} %shard_map.32), channel_id=1, source_target_pairs={{0,1},{1,0},{2,3},{3,2},{4,5},{5,4},{6,7},{7,6},{8,9},{9,8},{10,11... | collective-permute-start | bytes 2359304 | tf_op jit(solution)/shard_map/ppermute | solution.py:179
  87.5 24.3 %collective-permute-start.12 = (bf16[256,2048]{1,0:T(8,128)(2,1)S(1)}, bf16[256,2048]{1,0:T(8,128)(2,1)S(1)}, u32[]{:S(2)}, u32[]{:S(2)}) collective-permute-start(bf16[256,2048]{1,0:T(8,128)(2,1)S(1)} %get-tuple-element.244), channel_id=1, source_target_pairs={{0,6},{2,0},{4,2},{6,4},{8,14},{10,8},{12,10},{14,12},{16,22},{18,... | collective-permute-start | bytes 3145736 | tf_op jit(solution)/shard_map/ppermute | solution.py:195
  87.6 25.7 %collective-permute-start.13 = (bf16[256,2048]{1,0:T(8,128)(2,1)S(1)}, bf16[256,2048]{1,0:T(8,128)(2,1)S(1)}, u32[]{:S(2)}, u32[]{:S(2)}) collective-permute-start(bf16[256,2048]{1,0:T(8,128)(2,1)S(1)} %get-tuple-element.243), channel_id=1, source_target_pairs={{0,2},{2,4},{4,6},{6,0},{8,10},{10,12},{12,14},{14,8},{16,18},{18,... | collective-permute-start | bytes 3145736 | tf_op jit(solution)/shard_map/ppermute | solution.py:199
  101.7 32.6 %collective-permute-start.14 = (bf16[256,2048]{1,0:T(8,128)(2,1)S(1)}, bf16[256,2048]{1,0:T(8,128)(2,1)S(1)}, u32[]{:S(2)}, u32[]{:S(2)}) collective-permute-start(bf16[256,2048]{1,0:T(8,128)(2,1)S(1)} %get-tuple-element.242), channel_id=1, source_target_pairs={{0,6},{2,0},{4,2},{6,4},{8,14},{10,8},{12,10},{14,12},{16,22},{18,... | collective-permute-start | bytes 3145736 | tf_op jit(solution)/shard_map/ppermute | solution.py:195
  103.2 32.5 %collective-permute-start.15 = (bf16[256,2048]{1,0:T(8,128)(2,1)S(1)}, bf16[256,2048]{1,0:T(8,128)(2,1)S(1)}, u32[]{:S(2)}, u32[]{:S(2)}) collective-permute-start(bf16[256,2048]{1,0:T(8,128)(2,1)S(1)} %get-tuple-element.241), channel_id=1, source_target_pairs={{0,2},{2,4},{4,6},{6,0},{8,10},{10,12},{12,14},{14,8},{16,18},{18,... | collective-permute-start | bytes 3145736 | tf_op jit(solution)/shard_map/ppermute | solution.py:199
  113.2 6.8 %collective-permute-start.18 = (f32[512,384]{1,0:T(8,128)S(1)}, f32[512,384]{1,0:T(8,128)S(1)}, u32[]{:S(2)}, u32[]{:S(2)}) collective-permute-start(f32[512,384]{1,0:T(8,128)S(1)} %shard_map.36), channel_id=1, source_target_pairs={{0,1},{1,0},{2,3},{3,2},{4,5},{5,4},{6,7},{7,6},{8,9},{9,8},{10,11... | collective-permute-start | bytes 2359304 | tf_op jit(solution)/shard_map/ppermute | solution.py:179
  115.6 7.5 %collective-permute-start.17 = (f32[512,384]{1,0:T(8,128)S(1)}, f32[512,384]{1,0:T(8,128)S(1)}, u32[]{:S(2)}, u32[]{:S(2)}) collective-permute-start(f32[512,384]{1,0:T(8,128)S(1)} %shard_map.34), channel_id=1, source_target_pairs={{0,1},{1,0},{2,3},{3,2},{4,5},{5,4},{6,7},{7,6},{8,9},{9,8},{10,11... | collective-permute-start | bytes 2359304 | tf_op jit(solution)/shard_map/ppermute | solution.py:179
  115.6 10.7 %collective-permute-start.16 = (f32[512,384]{1,0:T(8,128)S(1)}, f32[512,384]{1,0:T(8,128)S(1)}, u32[]{:S(2)}, u32[]{:S(2)}) collective-permute-start(f32[512,384]{1,0:T(8,128)S(1)} %shard_map.35), channel_id=1, source_target_pairs={{0,1},{1,0},{2,3},{3,2},{4,5},{5,4},{6,7},{7,6},{8,9},{9,8},{10,11... | collective-permute-start | bytes 2359304 | tf_op jit(solution)/shard_map/ppermute | solution.py:179
  137.5 9.0 %collective-permute-start.20 = (f32[512,256]{1,0:T(8,128)S(1)}, f32[512,256]{1,0:T(8,128)S(1)}, u32[]{:S(2)}, u32[]{:S(2)}) collective-permute-start(f32[512,256]{1,0:T(8,128)S(1)} %get-tuple-element.213), channel_id=1, source_target_pairs={{0,1},{1,0},{2,3},{3,2},{4,5},{5,4},{6,7},{7,6},{8,9},{9,8},{10,11... | collective-permute-start | bytes 1572872 | tf_op jit(solution)/shard_map/ppermute | solution.py:179
  139.0 7.6 %collective-permute-start.21 = (f32[512,256]{1,0:T(8,128)S(1)}, f32[512,256]{1,0:T(8,128)S(1)}, u32[]{:S(2)}, u32[]{:S(2)}) collective-permute-start(f32[512,256]{1,0:T(8,128)S(1)} %get-tuple-element.214), channel_id=1, source_target_pairs={{0,1},{1,0},{2,3},{3,2},{4,5},{5,4},{6,7},{7,6},{8,9},{9,8},{10,11... | collective-permute-start | bytes 1572872 | tf_op jit(solution)/shard_map/ppermute | solution.py:179
  139.1 38.2 %collective-permute-start.26 = (bf16[384,2048]{1,0:T(8,128)(2,1)S(1)}, bf16[384,2048]{1,0:T(8,128)(2,1)S(1)}, u32[]{:S(2)}, u32[]{:S(2)}) collective-permute-start(bf16[384,2048]{1,0:T(8,128)(2,1)S(1)} %pad_maximum_fusion), channel_id=1, source_target_pairs={{0,126},{2,0},{4,2},{6,4},{8,6},{10,8},{12,10},{14,12},{16,14},{18... | collective-permute-start | bytes 4718600 | tf_op jit(solution)/shard_map/ppermute | solution.py:267
  144.0 2.6 %collective-permute-start.19 = (f32[512,128]{1,0:T(8,128)S(1)}, f32[512,128]{1,0:T(8,128)S(1)}, u32[]{:S(2)}, u32[]{:S(2)}) collective-permute-start(f32[512,128]{1,0:T(8,128)S(1)} %get-tuple-element.212), channel_id=1, source_target_pairs={{0,1},{1,0},{2,3},{3,2},{4,5},{5,4},{6,7},{7,6},{8,9},{9,8},{10,11... | collective-permute-start | bytes 786440 | tf_op jit(solution)/shard_map/ppermute | solution.py:179
  148.4 8.5 %collective-permute-start.24 = (f32[512,512]{1,0:T(8,128)S(1)}, f32[512,512]{1,0:T(8,128)S(1)}, u32[]{:S(2)}, u32[]{:S(2)}) collective-permute-start(f32[512,512]{1,0:T(8,128)S(1)} %shard_map.39), channel_id=1, source_target_pairs={{0,1},{1,0},{2,3},{3,2},{4,5},{5,4},{6,7},{7,6},{8,9},{9,8},{10,11... | collective-permute-start | bytes 3145736 | tf_op jit(solution)/shard_map/ppermute | solution.py:179
  148.5 11.6 %collective-permute-start.23 = (f32[512,512]{1,0:T(8,128)S(1)}, f32[512,512]{1,0:T(8,128)S(1)}, u32[]{:S(2)}, u32[]{:S(2)}) collective-permute-start(f32[512,512]{1,0:T(8,128)S(1)} %shard_map.46), channel_id=1, source_target_pairs={{0,1},{1,0},{2,3},{3,2},{4,5},{5,4},{6,7},{7,6},{8,9},{9,8},{10,11... | collective-permute-start | bytes 3145736 | tf_op jit(solution)/shard_map/ppermute | solution.py:179
  149.0 4.8 %collective-permute-start.25 = (f32[512,384]{1,0:T(8,128)S(1)}, f32[512,384]{1,0:T(8,128)S(1)}, u32[]{:S(2)}, u32[]{:S(2)}) collective-permute-start(f32[512,384]{1,0:T(8,128)S(1)} %shard_map.40), channel_id=1, source_target_pairs={{0,1},{1,0},{2,3},{3,2},{4,5},{5,4},{6,7},{7,6},{8,9},{9,8},{10,11... | collective-permute-start | bytes 2359304 | tf_op jit(solution)/shard_map/ppermute | solution.py:179
  149.1 35.8 %collective-permute-start.22 = (f32[512,640]{1,0:T(8,128)S(1)}, f32[512,640]{1,0:T(8,128)S(1)}, u32[]{:S(2)}, u32[]{:S(2)}) collective-permute-start(f32[512,640]{1,0:T(8,128)S(1)} %shard_map.45), channel_id=1, source_target_pairs={{0,2},{2,4},{4,6},{6,8},{8,10},{10,12},{12,14},{14,16},{16,18},{18... | collective-permute-start | bytes 3932168 | tf_op jit(solution)/shard_map/ppermute | solution.py:275
  178.8 3.2 %collective-permute-start.27 = (f32[512,384]{1,0:T(8,128)S(1)}, f32[512,384]{1,0:T(8,128)S(1)}, u32[]{:S(2)}, u32[]{:S(2)}) collective-permute-start(f32[512,384]{1,0:T(8,128)S(1)} %shard_map.50), channel_id=1, source_target_pairs={{0,1},{1,0},{2,3},{3,2},{4,5},{5,4},{6,7},{7,6},{8,9},{9,8},{10,11... | collective-permute-start | bytes 2359304 | tf_op jit(solution)/shard_map/ppermute | solution.py:179
  (1 other events, 0.9 us)
